TPU v7x, 32 devices: a whole 2x2x4 slice. The times are simulated.
32 devices in a mesh: group: 2 (over x), seq: 16 (over z, y, core).
Axes of the slice: x: 2, y: 2, z: 4, core: 2. Of those that a mesh axis runs over, the one named last changes fastest.
Arguments:
- queries: bfloat16 [4096, 4096], P(('group', 'seq')), parts along dimension 0, may hold values from -20 to 20
- response_keys: bfloat16 [4096, 512], P(('group', 'seq')), parts along dimension 0, may hold values from -6 to 6
- response_values: bfloat16 [4096, 512], P(('group', 'seq')), parts along dimension 0, may hold values from -6 to 6
- output_grad: bfloat16 [4096, 4096], P(('group', 'seq')), parts along dimension 0, may hold values from -6 to 6
- prompt_keys: bfloat16 [2048, 512], P(('group', 'seq')), parts along dimension 0, may hold values from -6 to 6
- prompt_values: bfloat16 [2048, 512], P(('group', 'seq')), parts along dimension 0, may hold values from -6 to 6
- block_list: int32 [32, 12], P('group'), parts along dimension 0, may hold values from 0 to 31, as said below
- block_count: int32 [32], P('group'), parts along dimension 0, may hold values from 6 to 12
- response_length: int32 [32], P(('group', 'seq')), parts along dimension 0, may hold values from 65 to 128
Outputs:
- output: bfloat16 [4096, 4096], P(('group', 'seq')), parts along dimension 0
- query_grad: bfloat16 [4096, 4096], P(('group', 'seq')), parts along dimension 0
- response_key_grad: bfloat16 [4096, 512], P(('group', 'seq')), parts along dimension 0
- response_value_grad: bfloat16 [4096, 512], P(('group', 'seq')), parts along dimension 0
- prompt_key_grad: bfloat16 [2048, 512], P(('group', 'seq')), parts along dimension 0
- prompt_value_grad: bfloat16 [2048, 512], P(('group', 'seq')), parts along dimension 0
There are 2 independent parts, one for each index of `group`. A program takes and returns all parts, laid end to end along the dimension named above; each array names one. Nothing has to cross between parts.
Inputs may be any that keep to these rules, and one draw needn't show every extreme that they name: `block_list`: each row names 12 different prompt blocks and at most one of the two blocks 2 p and 2 p + 1 that device p holds; entries at or after block_count of the row name blocks too but are not read.
All inputs are finite; a program needn't handle non-finite values.
Results may differ from a plain program's by a relative error of at most 0.022.
Values may be sent and summed in bfloat16 or wider, within the bound.
A program may use at most 64 MiB of HBM per device.

v0:
```python
import math

import jax
import jax.numpy as jnp
from jax import lax
from jax.sharding import PartitionSpec as P

HD = 128
QH = 32
KVH = 4


masked_score = -1e30


def attention(
    query_heads,
    grad_heads,
    prefix_keys,
    prefix_values,
    prefix_live,
    own_keys,
    own_values,
    self_visible,
):
    row_count, head_groups, group_size, head_width = query_heads.shape
    key_count = prefix_keys.shape[0]
    block_size = math.gcd(key_count, 256)
    block_total = key_count // block_size
    key_blocks = prefix_keys.reshape(block_total, block_size, head_groups, head_width)
    value_blocks = prefix_values.reshape(block_total, block_size, head_groups, head_width)
    live_blocks = prefix_live.reshape(block_total, 1, block_size)
    own_key_heads = own_keys.reshape(row_count, head_groups, head_width)
    own_value_heads = own_values.reshape(row_count, head_groups, head_width)
    scaling = 1.0 / math.sqrt(head_width)

    def masked_scores(key_heads, visible):
        scores = (
            jnp.einsum("tkgd,skd->kgts", query_heads, key_heads, preferred_element_type=jnp.float32)
            * scaling
        )
        return jnp.where(visible, scores, masked_score)

    def statistic_step(running, element):
        key_heads, visible = element
        row_max, row_total = running
        scores = masked_scores(key_heads, visible)
        new_max = jnp.maximum(row_max, scores.max(-1))
        row_total = row_total * jnp.exp(row_max - new_max) + jnp.exp(
            scores - new_max[..., None]
        ).sum(-1)
        return ((new_max, row_total), None)

    stat_shape = (head_groups, group_size, row_count)
    initial = (jnp.full(stat_shape, masked_score, jnp.float32), jnp.zeros(stat_shape, jnp.float32))
    running, _ = lax.scan(statistic_step, initial, (key_blocks, live_blocks))
    (row_max, row_total), _ = statistic_step(running, (own_key_heads, self_visible))

    def weights_of(key_heads, visible):
        return (
            jnp.exp(masked_scores(key_heads, visible) - row_max[..., None]) / row_total[..., None]
        )

    def output_step(accumulated, element):
        key_heads, value_heads, visible = element
        weights_low = weights_of(key_heads, visible).astype(jnp.bfloat16)
        update = jnp.einsum(
            "kgts,skd->tkgd", weights_low, value_heads, preferred_element_type=jnp.float32
        )
        return (accumulated + update, None)

    zeros_heads = jnp.zeros(query_heads.shape, jnp.float32)
    accumulated, _ = lax.scan(output_step, zeros_heads, (key_blocks, value_blocks, live_blocks))
    accumulated, _ = output_step(accumulated, (own_key_heads, own_value_heads, self_visible))
    output_heads = accumulated.astype(jnp.bfloat16)
    delta = jnp.einsum(
        "tkgd,tkgd->kgt", grad_heads, output_heads, preferred_element_type=jnp.float32
    )

    def gradient_step(accumulated, element):
        key_heads, value_heads, visible = element
        weights = weights_of(key_heads, visible)
        weights_low = weights.astype(jnp.bfloat16)
        weight_grad = jnp.einsum(
            "tkgd,skd->kgts", grad_heads, value_heads, preferred_element_type=jnp.float32
        )
        score_grad = (weights * (weight_grad - delta[..., None]) * scaling).astype(jnp.bfloat16)
        accumulated = accumulated + jnp.einsum(
            "kgts,skd->tkgd", score_grad, key_heads, preferred_element_type=jnp.float32
        )
        key_grad = jnp.einsum(
            "kgts,tkgd->skd", score_grad, query_heads, preferred_element_type=jnp.float32
        )
        value_grad = jnp.einsum(
            "kgts,tkgd->skd", weights_low, grad_heads, preferred_element_type=jnp.float32
        )
        return (accumulated, (key_grad, value_grad))

    accumulated, (key_terms, value_terms) = lax.scan(
        gradient_step, zeros_heads, (key_blocks, value_blocks, live_blocks)
    )
    accumulated, (own_key_terms, own_value_terms) = gradient_step(
        accumulated, (own_key_heads, own_value_heads, self_visible)
    )
    return (
        output_heads.reshape(row_count, -1),
        accumulated.astype(jnp.bfloat16).reshape(row_count, -1),
        own_key_terms.reshape(row_count, -1),
        own_value_terms.reshape(row_count, -1),
        key_terms.reshape(key_count, -1),
        value_terms.reshape(key_count, -1),
    )


def per_device(
    queries,
    response_keys,
    response_values,
    output_grad,
    prompt_keys,
    prompt_values,
    block_list,
    block_count,
    response_length,
):
    row_count = queries.shape[0]
    device_count = lax.axis_size("seq")
    device_index = lax.axis_index("seq")
    group_size = QH // KVH
    query_heads = queries.reshape(row_count, KVH, group_size, HD)
    positions = jnp.arange(row_count)
    live_length = response_length[0]
    row_live = positions < live_length
    live_grad = jnp.where(row_live[:, None], output_grad, jnp.zeros_like(output_grad))
    grad_heads = live_grad.reshape(row_count, KVH, group_size, HD)
    self_visible = (positions[None, :] <= positions[:, None]) & (positions[None, :] < live_length)
    listed_ids = lax.dynamic_index_in_dim(block_list, device_index, 0, keepdims=False)
    listed_count = lax.dynamic_index_in_dim(block_count, device_index, 0, keepdims=False)
    slot_count = block_list.shape[1]
    entry_live = jnp.arange(slot_count) < listed_count
    block_rows = prompt_keys.shape[0] // 2
    all_keys, all_values = (
        lax.all_gather(prompt_keys, "seq", axis=0, tiled=True),
        lax.all_gather(prompt_values, "seq", axis=0, tiled=True),
    )
    block_index = jnp.arange(2 * device_count)
    visible_blocks = ((listed_ids[:, None] == block_index[None, :]) & entry_live[:, None]).any(0)
    prefix_live = jnp.repeat(visible_blocks, block_rows)
    results = attention(
        query_heads,
        grad_heads,
        all_keys,
        all_values,
        prefix_live,
        response_keys,
        response_values,
        self_visible,
    )
    key_share = results[4].astype(jnp.bfloat16)
    value_share = results[5].astype(jnp.bfloat16)
    prompt_key_grad, prompt_value_grad = (
        lax.psum_scatter(key_share, "seq", scatter_dimension=0, tiled=True).astype(jnp.float32),
        lax.psum_scatter(value_share, "seq", scatter_dimension=0, tiled=True).astype(jnp.float32),
    )
    return (
        results[0],
        results[1],
        results[2].astype(jnp.bfloat16),
        results[3].astype(jnp.bfloat16),
        prompt_key_grad.astype(jnp.bfloat16),
        prompt_value_grad.astype(jnp.bfloat16),
    )


def solution(mesh):
    return jax.shard_map(
        per_device,
        mesh=mesh,
        in_specs=(
            P(("group", "seq"), None),
            P(("group", "seq"), None),
            P(("group", "seq"), None),
            P(("group", "seq"), None),
            P(("group", "seq"), None),
            P(("group", "seq"), None),
            P("group", None),
            P("group"),
            P(("group", "seq")),
        ),
        out_specs=(
            P(("group", "seq"), None),
            P(("group", "seq"), None),
            P(("group", "seq"), None),
            P(("group", "seq"), None),
            P(("group", "seq"), None),
            P(("group", "seq"), None),
        ),
        check_vma=False,
    )
```

profile of v0, /device:TPU:0, one launch (start us, length us, event | category | flops | bytes accessed | tf_op | source)
XLA Modules:
  0.0 288.7 jit_solution(4933074256335214968)
XLA Ops:
  12.9 1.6 reshape.85
  14.5 1.7 copy.72
  18.5 1.7 fusion.57
  20.3 30.6 %all-gather.5.cloned.1.call-done = bf16[1024,512]{1,0:T(8,128)(2,1)} async-done(((bf16[64,512]{1,0:T(8,128)(2,1)}), bf16[1024,512]{1,0:T(8,128)(2,1)}) %all-gather.5.cloned.1.call-update) | async-done | bytes 1048592 | tf_op jit(solution)/shard_map/all_gather | solution.py:143
  50.9 2.1 reshape.82
  53.0 2.4 copy.80
  55.4 11.2 %while.39 = (s32[]{:T(128)}, f32[4,8,128]{2,1,0:T(8,128)S(1)}, f32[4,8,128]{2,1,0:T(8,128)S(1)}, pred[4,1,256]{2,1,0:T(4,128)(4,1)S(1)}, bf16[4,256,4,128]{3,1,2...) while((s32[]{:T(128)}, f32[4,8,128]{2,1,0:T(8,128)S(1)}, ...), condition=%wide.region_4.5_spmd.clone, body=%wide.region_1.4_spmd.clone.sunk | while | flops 275795968 | bytes 9913456 | solution.py:56
  55.4 1.7 bitcast_reduce_fusion.2
  58.2 1.7 bitcast_reduce_fusion.2
  61.0 1.7 bitcast_reduce_fusion.2
  63.8 1.7 bitcast_reduce_fusion.2
  67.6 22.3 %all-gather.3.cloned.1.call-done = bf16[1024,512]{1,0:T(8,128)(2,1)} async-done(((bf16[64,512]{1,0:T(8,128)(2,1)}), bf16[1024,512]{1,0:T(8,128)(2,1)}) %all-gather.3.cloned.1.call-update) | async-done | bytes 1048592 | tf_op jit(solution)/shard_map/all_gather | solution.py:144
  89.9 2.1 reshape.81
  92.0 28.5 %while.40 = (s32[]{:T(128)}, f32[128,4,8,128]{0,3,2,1:T(8,128)}, bf16[4,256,4,128]{3,2,1,0:T(4,128)(2,1)}, pred[4,1,256]{2,1,0:T(4,128)(4,1)S(1)}, bf16[4,256,4,...) while((s32[]{:T(128)}, f32[128,4,8,128]{0,3,2,1:T(8,128)}, ...), condition=%wide.region_8.9_spmd.clone, body=%wide.region_7.8_spmd.clone.sunk | while | flops 543162368 | bytes 6980539 | solution.py:73
  94.6 4.0 %bitcast_add_fusion.6 = f32[128,4,8,128]{0,3,2,1:T(8,128)} fusion(f32[128,4,8,128]{0,3,2,1:T(8,128)} %get-tuple-element.573, bf16[128,4,8,128]{3,0,2,1:T(8,128)(2,1)S(1)} %get-tuple-element.587, f32[4,8,128]{2,1,0:T(8,128)} %get-tuple-element.589, f32[4,8,128]{2,1,0:T(8,128)} %copy-done.17, pred[256]{0:T(512)(128)(4,1)S(1)} %dynamic-slice_reduce_fusion.7, ...), kind=kOutput, calls=%fused_computation.17.clone.1 | convolution fusion | flops 543162368 | bytes 5800197 | tf_op jit(solution)/shard_map/while/body/eval_jaxpr/kgts,skd->tkgd/dot_general | solution.py:67
  101.1 4.8 %bitcast_add_fusion.6 = f32[128,4,8,128]{0,3,2,1:T(8,128)} fusion(f32[128,4,8,128]{0,3,2,1:T(8,128)} %get-tuple-element.573, bf16[128,4,8,128]{3,0,2,1:T(8,128)(2,1)S(1)} %get-tuple-element.587, f32[4,8,128]{2,1,0:T(8,128)} %get-tuple-element.589, f32[4,8,128]{2,1,0:T(8,128)} %copy-done.17, pred[256]{0:T(512)(128)(4,1)S(1)} %dynamic-slice_reduce_fusion.7, ...), kind=kOutput, calls=%fused_computation.17.clone.1 | convolution fusion | flops 543162368 | bytes 5800197 | tf_op jit(solution)/shard_map/while/body/eval_jaxpr/kgts,skd->tkgd/dot_general | solution.py:67
  108.5 4.8 %bitcast_add_fusion.6 = f32[128,4,8,128]{0,3,2,1:T(8,128)} fusion(f32[128,4,8,128]{0,3,2,1:T(8,128)} %get-tuple-element.573, bf16[128,4,8,128]{3,0,2,1:T(8,128)(2,1)S(1)} %get-tuple-element.587, f32[4,8,128]{2,1,0:T(8,128)} %get-tuple-element.589, f32[4,8,128]{2,1,0:T(8,128)} %copy-done.17, pred[256]{0:T(512)(128)(4,1)S(1)} %dynamic-slice_reduce_fusion.7, ...), kind=kOutput, calls=%fused_computation.17.clone.1 | convolution fusion | flops 543162368 | bytes 5800197 | tf_op jit(solution)/shard_map/while/body/eval_jaxpr/kgts,skd->tkgd/dot_general | solution.py:67
  115.8 4.8 %bitcast_add_fusion.6 = f32[128,4,8,128]{0,3,2,1:T(8,128)} fusion(f32[128,4,8,128]{0,3,2,1:T(8,128)} %get-tuple-element.573, bf16[128,4,8,128]{3,0,2,1:T(8,128)(2,1)S(1)} %get-tuple-element.587, f32[4,8,128]{2,1,0:T(8,128)} %get-tuple-element.589, f32[4,8,128]{2,1,0:T(8,128)} %copy-done.17, pred[256]{0:T(512)(128)(4,1)S(1)} %dynamic-slice_reduce_fusion.7, ...), kind=kOutput, calls=%fused_computation.17.clone.1 | convolution fusion | flops 543162368 | bytes 5800197 | tf_op jit(solution)/shard_map/while/body/eval_jaxpr/kgts,skd->tkgd/dot_general | solution.py:67
  120.5 4.3 %fusion.43 = (f32[4,8,128]{2,1,0:T(8,128)S(1)}, bf16[128,4096]{0,1:T(8,128)(2,1)}, bf16[128,4,8,128]{0,3,2,1:T(8,128)(2,1)}) fusion(bf16[128,4096]{0,1:T(8,128)(2,1)} %copy.84, pred[128]{0:T(512)(128)(4,1)} %copy-done.22, f32[128,4,8,128]{0,3,2,1:T(8,128)} %get-tuple-element.147, f32[4,8,128]{2,1,0:T(8,128)} %get-tuple-element.654, ...), kind=kOutput, calls=%fused_computation.56 | convolution fusion | flops 139456512 | bytes 7520384 | tf_op jit(solution)/shard_map/kgts,skd->tkgd/dot_general | solution.py:67
  124.9 1.7 copy.89
  126.6 34.9 %while.41 = (s32[]{:T(128)}, f32[128,4,8,128]{0,3,2,1:T(8,128)}, bf16[4,256,4,128]{3,1,2,0:T(8,128)(2,1)}, bf16[4,256,4,128]{3,1,2,0:T(8,128)(2,1)}, bf16[4,256,...) while((s32[]{:T(128)}, f32[128,4,8,128]{0,3,2,1:T(8,128)}, ...), condition=%wide.region_10.11_spmd.clone, body=%wide.region_9.10_spmd.clone.sunk | while | flops 1352663040 | bytes 63227220 | solution.py:99
  134.0 1.3 copy-done.2
  142.8 1.3 copy-done.2
  151.5 1.3 copy-done.2
  161.5 2.0 copy.98
  167.3 1.3 copy.99
  168.9 2.1 fusion.42
  172.2 2.6 fusion.48
  175.6 1.4 fusion.39
  176.9 2.3 copy.100
  179.2 42.0 %reduce-scatter.5.cloned.1.call-done = bf16[64,512]{1,0:T(8,128)(2,1)} async-done(((bf16[1024,512]{1,0:T(8,128)(2,1)}), bf16[64,512]{1,0:T(8,128)(2,1)}) %reduce-scatter.5.cloned.1.call-update) | async-done | bytes 65552 | tf_op jit(solution)/shard_map/reduce_scatter | solution.py:163
  221.2 60.9 %reduce-scatter.3.cloned.1.call-done = bf16[64,512]{1,0:T(8,128)(2,1)} async-done(((bf16[1024,512]{1,0:T(8,128)(2,1)}), bf16[64,512]{1,0:T(8,128)(2,1)}) %reduce-scatter.3.cloned.1.call-update) | async-done | bytes 65552 | tf_op jit(solution)/shard_map/reduce_scatter | solution.py:162
  (187 shorter events, 59.3 us)
Async XLA Ops:
  7.2 4.2 %copy-start = (s32[16,12]{1,0:T(8,128)S(1)}, s32[16,12]{1,0:T(8,128)}, u32[]{:S(2)}) copy-start(s32[16,12]{1,0:T(8,128)} %param.21) | copy-start | bytes 2308
  7.2 43.7 %all-gather.5.cloned.1.call-start = ((), (), s32[]{:S(2)}) async-start(), calls=%async_computation.3 | async-start | bytes 1114112 | tf_op jit(solution)/shard_map/all_gather | solution.py:143
  7.9 82.0 %all-gather.3.cloned.1.call-start = ((), (), s32[]{:S(2)}) async-start(), calls=%async_computation.2 | async-start | bytes 1114112 | tf_op jit(solution)/shard_map/all_gather | solution.py:144
  8.7 212.5 %reduce-scatter.5.cloned.1.call-start = ((), (), s32[]{:S(2)}) async-start(), calls=%async_computation.5 | async-start | bytes 1114112 | tf_op jit(solution)/shard_map/reduce_scatter | solution.py:163
  9.4 2.3 copy-start.22
  14.5 2.7 copy-start.10
  20.3 100.3 %copy-start.4 = (f32[4,8,128,128]{2,3,1,0:T(8,128)}, f32[4,8,128,128]{2,3,1,0:T(8,128)S(1)}, u32[]{:S(2)}) copy-start(f32[4,8,128,128]{2,3,1,0:T(8,128)S(1)} %get-tuple-element.373) | copy-start | bytes 6291460
  94.6 4.0 %copy-start.18 = (f32[4,8,128]{2,1,0:T(8,128)S(1)}, f32[4,8,128]{2,1,0:T(8,128)}, u32[]{:S(2)}) copy-start(f32[4,8,128]{2,1,0:T(8,128)} %copy-done.17) | copy-start | bytes 49156 | tf_op jit(solution)/shard_map/while
  101.1 4.8 %copy-start.18 = (f32[4,8,128]{2,1,0:T(8,128)S(1)}, f32[4,8,128]{2,1,0:T(8,128)}, u32[]{:S(2)}) copy-start(f32[4,8,128]{2,1,0:T(8,128)} %copy-done.17) | copy-start | bytes 49156 | tf_op jit(solution)/shard_map/while
  108.5 4.8 %copy-start.18 = (f32[4,8,128]{2,1,0:T(8,128)S(1)}, f32[4,8,128]{2,1,0:T(8,128)}, u32[]{:S(2)}) copy-start(f32[4,8,128]{2,1,0:T(8,128)} %copy-done.17) | copy-start | bytes 49156 | tf_op jit(solution)/shard_map/while
  115.8 4.8 %copy-start.18 = (f32[4,8,128]{2,1,0:T(8,128)S(1)}, f32[4,8,128]{2,1,0:T(8,128)}, u32[]{:S(2)}) copy-start(f32[4,8,128]{2,1,0:T(8,128)} %copy-done.17) | copy-start | bytes 49156 | tf_op jit(solution)/shard_map/while
  124.9 1.7 copy-start.8
  124.9 1.7 copy-start.21
  129.8 1.6 copy-start.13
  131.4 1.6 copy-start.1
  134.0 1.3 copy-start.2
  138.5 1.6 copy-start.13
  140.1 1.6 copy-start.1
  147.2 1.6 copy-start.13
  148.8 1.6 copy-start.1
  151.5 1.3 copy-start.2
  155.9 1.6 copy-start.13
  157.6 1.6 copy-start.1
  161.5 3.2 %copy-start.19 = (f32[4,8,128]{2,1,0:T(8,128)}, f32[4,8,128]{2,1,0:T(8,128)S(1)}, u32[]{:S(2)}) copy-start(f32[4,8,128]{2,1,0:T(8,128)S(1)} %get-tuple-element.651) | copy-start | bytes 49156
  163.6 1.5 copy-start.15
  164.7 117.4 %reduce-scatter.3.cloned.1.call-start = ((), (), s32[]{:S(2)}) async-start(), calls=%async_computation.4 | async-start | bytes 1114112 | tf_op jit(solution)/shard_map/reduce_scatter | solution.py:162
  165.9 1.5 copy-start.9
  167.1 1.8 copy-start.5
  167.1 1.8 copy-start.16
  167.1 1.8 copy-start.20
  168.9 2.1 copy-start.7
  172.2 3.4 %copy-start.3 = (f32[128,4,8,128]{0,3,2,1:T(8,128)S(1)}, f32[128,4,8,128]{0,3,2,1:T(8,128)}, u32[]{:S(2)}) copy-start(f32[128,4,8,128]{0,3,2,1:T(8,128)} %get-tuple-element.148) | copy-start | bytes 6291460
  (19 other events, 19.0 us)
Sparse Core Ops, SparseCore 0:
  10.2 40.6 all-gather.4
  53.0 36.8 all-gather.2
  164.9 56.3 reduce-scatter.4
  225.7 56.3 reduce-scatter.2
where the time goes:
time: 290 us; the launch traced here: 289 us
  waiting for transfers between devices  157 us (54%)
  matrix products  56.2 us (19%)
  local copies, waits for them, and re-layouts  54 us (19%)
  between operations  14.7 us (5%)
  other arithmetic  5.92 us (2%)
    reduce_scatter x1, waiting for transfers between devices, per_device(): lax.psum_scatter(key_share, 'seq', scatter_dimension=0, tiled=True)  60.9 us
    reduce_scatter x1, waiting for transfers between devices, per_device(): lax.psum_scatter(value_share, 'seq', scatter_dimension=0, tiled=True)  42 us
    all_gather x1, waiting for transfers between devices, per_device(): lax.all_gather(prompt_keys, 'seq', axis=0, tiled=True)  30.6 us
    dot_general x5, matrix products, output_step(): jnp.einsum('kgts,skd->tkgd', weights_low, value_heads, preferred_element_...  22.6 us
    all_gather x1, waiting for transfers between devices, per_device(): lax.all_gather(prompt_values, 'seq', axis=0, tiled=True)  22.3 us
    unnamed x41, local copies, waits for them, and re-layouts  16.3 us
    while x68, local copies, waits for them, and re-layouts  14.2 us
    dot_general x9, matrix products, masked_scores(): jnp.einsum('tkgd,skd->kgts', query_heads, key_heads, preferred_element_ty...  13.3 us
  transfers between devices with their start and end apart: 4, of which 4 were waited for; matrix products, arithmetic and copies ran while one was open for 14% of the time, Pallas kernels for 0%

commit v1 on v0

v1 whole, which is shorter than its diff:
```python
import functools
import math

import jax
import jax.numpy as jnp
from jax import lax
from jax.experimental import pallas as pl
from jax.experimental.pallas import tpu as pltpu
from jax.sharding import PartitionSpec as P

HD = 128
QH = 32
KVH = 4
GROUP = QH // KVH

MASKED = -1e30


def dot(a, b, ca=1, cb=0):
    return lax.dot_general(
        a, b, (((ca,), (cb,)), ((), ())), preferred_element_type=jnp.float32
    )


def attention_kernel(
    block_rows,
    slots_ref,
    meta_ref,
    q_ref,
    do_ref,
    pk_ref,
    pv_ref,
    ok_ref,
    ov_ref,
    out_ref,
    dq_ref,
    dok_ref,
    dov_ref,
    dpk_ref,
    dpv_ref,
    k_all,
    v_all,
    bias,
    ds_all,
    wl_all,
    q_all,
    do_all,
):
    rows = q_ref.shape[0]
    entries = slots_ref.shape[0]
    prefix = entries * block_rows
    keys = prefix + rows
    scaling = 1.0 / math.sqrt(HD)
    count, length = meta_ref[0], meta_ref[1]

    @pl.when(pl.program_id(0) == 0)
    def _():
        key_row = lax.broadcasted_iota(jnp.int32, (prefix, 2 * rows), 0)
        bias[:prefix, :] = jnp.where(key_row < count * block_rows, 0.0, MASKED)
        own = lax.broadcasted_iota(jnp.int32, (rows, rows), 0)
        tok = lax.broadcasted_iota(jnp.int32, (rows, rows), 1)
        own_bias = jnp.where((own <= tok) & (own < length), 0.0, MASKED)
        bias[prefix:, :rows] = own_bias
        bias[prefix:, rows:] = own_bias

    for i in range(entries):
        start = pl.multiple_of(slots_ref[i] * block_rows, block_rows)
        k_all[i * block_rows : (i + 1) * block_rows, :] = pk_ref[pl.ds(start, block_rows), :]
        v_all[i * block_rows : (i + 1) * block_rows, :] = pv_ref[pl.ds(start, block_rows), :]
    k_all[prefix:, :] = ok_ref[...]
    v_all[prefix:, :] = ov_ref[...]
    kk, vv = k_all[...], v_all[...]
    kt, vt = kk.T, vv.T
    live = (lax.broadcasted_iota(jnp.int32, (rows, HD), 0) < length).astype(jnp.float32)
    live = live.astype(jnp.bfloat16)
    for h in range(GROUP):
        q_all[h * rows : (h + 1) * rows, :] = q_ref[:, h * HD : (h + 1) * HD]
        do_all[h * rows : (h + 1) * rows, :] = do_ref[:, h * HD : (h + 1) * HD] * live
    for pair in range(GROUP // 2):
        span = slice(pair * 2 * rows, (pair + 1) * 2 * rows)
        q2, do2 = q_all[span, :], do_all[span, :]
        do2t = do2.T
        s = dot(kk, q2, 1, 1) * (scaling * math.log2(math.e)) + bias[...]
        e = jnp.exp2(s - s.max(0, keepdims=True))
        w = e * (1.0 / e.sum(0, keepdims=True))
        wl = w.astype(jnp.bfloat16)
        wl_all[:, span] = wl
        ot = dot(vt, wl).astype(jnp.bfloat16)
        delta = (do2t.astype(jnp.float32) * ot.astype(jnp.float32)).sum(0, keepdims=True)
        dp = dot(vv, do2t)
        ds = (w * (dp - delta) * scaling).astype(jnp.bfloat16)
        ds_all[:, span] = ds
        dqt = dot(kt, ds).astype(jnp.bfloat16)
        for j in range(2):
            h = 2 * pair + j
            out_ref[:, h * HD : (h + 1) * HD] = ot[:, j * rows : (j + 1) * rows].T
            dq_ref[:, h * HD : (h + 1) * HD] = dqt[:, j * rows : (j + 1) * rows].T
    dk = dot(ds_all[...], q_all[...]).astype(jnp.bfloat16)
    dv = dot(wl_all[...], do_all[...]).astype(jnp.bfloat16)
    dok_ref[...] = dk[prefix:, :]
    dov_ref[...] = dv[prefix:, :]
    dpk_ref[...] = jnp.zeros_like(dpk_ref)
    dpv_ref[...] = jnp.zeros_like(dpv_ref)
    for i in range(entries):
        start = pl.multiple_of(slots_ref[i] * block_rows, block_rows)
        dpk_ref[pl.ds(start, block_rows), :] = dk[i * block_rows : (i + 1) * block_rows, :]
        dpv_ref[pl.ds(start, block_rows), :] = dv[i * block_rows : (i + 1) * block_rows, :]


def attention(slots, meta, queries, grads, keys, values, own_keys, own_values, block_rows):
    rows, width = queries.shape
    slot_rows = keys.shape[0]
    total = slots.shape[0] * block_rows + rows
    wide = pl.BlockSpec((rows, GROUP * HD), lambda g, *_: (0, g))
    own = pl.BlockSpec((rows, HD), lambda g, *_: (0, g))
    prompt = pl.BlockSpec((slot_rows, HD), lambda g, *_: (0, g))
    low = jnp.bfloat16
    return pl.pallas_call(
        functools.partial(attention_kernel, block_rows),
        grid_spec=pltpu.PrefetchScalarGridSpec(
            num_scalar_prefetch=2,
            grid=(KVH,),
            in_specs=[wide, wide, prompt, prompt, own, own],
            out_specs=[wide, wide, own, own, prompt, prompt],
            scratch_shapes=[
                pltpu.VMEM((total, HD), low),
                pltpu.VMEM((total, HD), low),
                pltpu.VMEM((total, 2 * rows), jnp.float32),
                pltpu.VMEM((total, GROUP * rows), low),
                pltpu.VMEM((total, GROUP * rows), low),
                pltpu.VMEM((GROUP * rows, HD), low),
                pltpu.VMEM((GROUP * rows, HD), low),
            ],
        ),
        out_shape=[
            jax.ShapeDtypeStruct((rows, width), low),
            jax.ShapeDtypeStruct((rows, width), low),
            jax.ShapeDtypeStruct((rows, KVH * HD), low),
            jax.ShapeDtypeStruct((rows, KVH * HD), low),
            jax.ShapeDtypeStruct((slot_rows, KVH * HD), low),
            jax.ShapeDtypeStruct((slot_rows, KVH * HD), low),
        ],
        compiler_params=pltpu.CompilerParams(vmem_limit_bytes=40 << 20),
        name="attention",
    )(slots, meta, queries, grads, keys, values, own_keys, own_values)


def per_device(
    queries,
    response_keys,
    response_values,
    output_grad,
    prompt_keys,
    prompt_values,
    block_list,
    block_count,
    response_length,
):
    device_index = lax.axis_index("seq")
    listed = lax.dynamic_index_in_dim(block_list, device_index, 0, keepdims=False)
    count = lax.dynamic_index_in_dim(block_count, device_index, 0, keepdims=True)
    meta = jnp.concatenate([count, response_length])
    block_rows = prompt_keys.shape[0] // 2
    all_keys = lax.all_gather(prompt_keys, "seq", axis=0, tiled=True)
    all_values = lax.all_gather(prompt_values, "seq", axis=0, tiled=True)
    out, dq, dok, dov, dpk, dpv = attention(
        listed, meta, queries, output_grad, all_keys, all_values, response_keys, response_values, block_rows
    )
    return (
        out,
        dq,
        dok,
        dov,
        lax.psum_scatter(dpk, "seq", scatter_dimension=0, tiled=True),
        lax.psum_scatter(dpv, "seq", scatter_dimension=0, tiled=True),
    )


def solution(mesh):
    both = P(("group", "seq"), None)
    return jax.shard_map(
        per_device,
        mesh=mesh,
        in_specs=(both, both, both, both, both, both, P("group", None), P("group"), P(("group", "seq"))),
        out_specs=(both,) * 6,
        check_vma=False,
    )
```

time: 290 us -> 238 us (0.82)
  matrix products: 56.2 us -> 0 us
  local copies, waits for them, and re-layouts: 54 us -> 7.05 us
  waiting for transfers between devices: 157 us -> 197 us
  Pallas kernels: 0 us -> 18 us
  other arithmetic: 5.92 us -> 0.72 us
    dot_general x34 -> x0, matrix products: 56.2 us -> none  [the longest x5 22.6 us: output_step(): jnp.einsum('kgts,skd->tkgd', weights_low, value_heads, preferred_element_...]
    all_gather x2, waiting for transfers between devices: 52.9 us -> 78.6 us  [the longest x1 39.5 us: per_device(): all_keys = lax.all_gather(prompt_keys, 'seq', axis=0, tiled=True)]
    pallas_call x0 -> x1, Pallas kernels: none -> 18 us  [attention(): pl.pallas_call(functools.partial(attention_kernel, block_rows), grid_spec...]
    while x68 -> x0, local copies, waits for them, and re-layouts: 14.2 us -> none
    reduce_scatter x2, waiting for transfers between devices: 103 us -> 117 us  [the longest x1 60.9 us: per_device(): lax.psum_scatter(dpv, 'seq', scatter_dimension=0, tiled=True)]
    dynamic_slice x25 -> x1, local copies, waits for them, and re-layouts: 13.4 us -> 0.58 us  [per_device(): lax.dynamic_index_in_dim(block_count, device_index, 0, keepdims=True)]
    unnamed x41 -> x16, local copies, waits for them, and re-layouts: 16.3 us -> 6.46 us
    reshape x5 -> x0, local copies, waits for them, and re-layouts: 6.94 us -> none  [the longest x1 2.13 us: attention(): prefix_keys.reshape(block_total, block_size, head_groups, head_width)]
  transfers between devices with their start and end apart: 4 -> 4, of which waited for: 4 -> 4; matrix products, arithmetic and copies ran while one was open for 14% -> 1% of each run, Pallas kernels for 0% -> 0%
where the time goes in v1:
time: 238 us
  waiting for transfers between devices  197 us (83%)
  Pallas kernels  18 us (8%)
  between operations  14.4 us (6%)
  local copies, waits for them, and re-layouts  7.05 us (3%)
    reduce_scatter x1, waiting for transfers between devices, per_device(): lax.psum_scatter(dpv, 'seq', scatter_dimension=0, tiled=True)  60.9 us
    reduce_scatter x1, waiting for transfers between devices, per_device(): lax.psum_scatter(dpk, 'seq', scatter_dimension=0, tiled=True)  55.9 us
    all_gather x1, waiting for transfers between devices, per_device(): all_keys = lax.all_gather(prompt_keys, 'seq', axis=0, tiled=True)  39.5 us
    all_gather x1, waiting for transfers between devices, per_device(): all_values = lax.all_gather(prompt_values, 'seq', axis=0, tiled=True)  39 us
    pallas_call x1, Pallas kernels, attention(): pl.pallas_call(functools.partial(attention_kernel, block_rows), grid_spec...  18 us
    unnamed x16, local copies, waits for them, and re-layouts  6.46 us
  transfers between devices with their start and end apart: 4, of which 4 were waited for; matrix products, arithmetic and copies ran while one was open for 1% of the time, Pallas kernels for 0%

profile of v1, /device:TPU:0, one launch (start us, length us, event | category | flops | bytes accessed | tf_op | source)
XLA Modules:
  0.0 237.7 jit_solution(18042231016993157769)
XLA Ops:
  7.2 0.0 copy-start
  7.2 0.0 copy-start.5
  7.2 0.0 all-gather.3.cloned.1.call-start
  7.2 0.7 all-gather.3.cloned.1.call-update
  7.9 0.0 all-gather.5.cloned.1.call-start
  8.0 0.7 all-gather.5.cloned.1.call-update
  8.7 0.0 reduce-scatter.3.cloned.1.call-start
  9.4 0.0 copy-start.7
  9.4 0.6 copy-done.7
  10.0 0.6 dynamic_slice.9
  10.6 0.0 copy-done
  10.6 0.7 pad_add_fusion.meta_ref
  11.3 39.5 %all-gather.3.cloned.1.call-done.pk_ref = bf16[1024,512]{1,0:T(8,128)(2,1)} async-done(((bf16[64,512]{1,0:T(8,128)(2,1)}), bf16[1024,512]{1,0:T(8,128)(2,1)}) %all-gather.3.cloned.1.call-update) | async-done | bytes 1048592 | tf_op jit(solution)/shard_map/all_gather | solution.py:164
  50.9 39.0 %all-gather.5.cloned.1.call-done.pv_ref = bf16[1024,512]{1,0:T(8,128)(2,1)} async-done(((bf16[64,512]{1,0:T(8,128)(2,1)}), bf16[1024,512]{1,0:T(8,128)(2,1)}) %all-gather.5.cloned.1.call-update) | async-done | bytes 1048592 | tf_op jit(solution)/shard_map/all_gather | solution.py:165
  89.9 0.0 copy-done.5
  89.9 0.0 copy-start.1
  89.9 1.2 copy-done.1
  91.1 0.0 copy-start.2
  91.1 1.2 copy-done.2
  92.4 0.0 copy-start.3
  92.4 1.2 copy-done.3
  93.6 0.0 copy-start.4
  93.6 1.2 copy-done.4
  94.8 0.0 copy-start.6
  94.8 0.9 copy-done.6
  95.7 18.0 %attention.1 = (bf16[128,4096]{1,0:T(8,128)(2,1)}, bf16[128,4096]{1,0:T(8,128)(2,1)}, bf16[128,512]{1,0:T(8,128)(2,1)}, bf16[128,512]{1,0:T(8,128)(2,1)}, bf16[1...) custom-call(s32[12]{0:T(128)S(1)} %dynamic-slice_bitcast_fusion.slots_ref, s32[2]{0:T(128)S(1)} %pad_add_fusion.meta_ref, ...), custom_call_target="tpu_custom_call" | custom-call | tf_op jit(solution)/shard_map/attention/pallas_call | solution.py:118
  113.7 0.0 reduce-scatter.3.cloned.1.call-update
  113.8 0.0 reduce-scatter.5.cloned.1.call-start
  113.8 0.5 reduce-scatter.5.cloned.1.call-update
  114.3 55.9 %reduce-scatter.3.cloned.1.call-done = bf16[64,512]{1,0:T(8,128)(2,1)} async-done(((bf16[1024,512]{1,0:T(8,128)(2,1)}), bf16[64,512]{1,0:T(8,128)(2,1)}) %reduce-scatter.3.cloned.1.call-update) | async-done | bytes 65552 | tf_op jit(solution)/shard_map/reduce_scatter | solution.py:174
  170.2 60.9 %reduce-scatter.5.cloned.1.call-done = bf16[64,512]{1,0:T(8,128)(2,1)} async-done(((bf16[1024,512]{1,0:T(8,128)(2,1)}), bf16[64,512]{1,0:T(8,128)(2,1)}) %reduce-scatter.5.cloned.1.call-update) | async-done | bytes 65552 | tf_op jit(solution)/shard_map/reduce_scatter | solution.py:175
  (1 shorter events, 0.0 us)
Async XLA Ops:
  7.2 3.4 %copy-start = (s32[16,12]{1,0:T(8,128)S(1)}, s32[16,12]{1,0:T(8,128)}, u32[]{:S(2)}) copy-start(s32[16,12]{1,0:T(8,128)} %param.15) | copy-start | bytes 2308
  7.2 82.7 %copy-start.5 = (bf16[128,512]{1,0:T(8,128)(2,1)S(1)}, bf16[128,512]{1,0:T(8,128)(2,1)}, u32[]{:S(2)}) copy-start(bf16[128,512]{1,0:T(8,128)(2,1)} %ok_ref.1) | copy-start | bytes 393220
  7.2 43.7 %all-gather.3.cloned.1.call-start = ((), (), s32[]{:S(2)}) async-start(), calls=%async_computation.2 | async-start | bytes 1114112 | tf_op jit(solution)/shard_map/all_gather | solution.py:164
  7.9 82.0 %all-gather.5.cloned.1.call-start = ((), (), s32[]{:S(2)}) async-start(), calls=%async_computation.3 | async-start | bytes 1114112 | tf_op jit(solution)/shard_map/all_gather | solution.py:165
  8.7 161.6 %reduce-scatter.3.cloned.1.call-start = ((), (), s32[]{:S(2)}) async-start(), calls=%async_computation.4 | async-start | bytes 1114112 | tf_op jit(solution)/shard_map/reduce_scatter | solution.py:174
  9.4 0.7 copy-start.7
  89.9 1.2 copy-start.1
  91.1 1.2 copy-start.2
  92.4 1.2 copy-start.3
  93.6 1.2 copy-start.4
  94.8 0.9 copy-start.6
  113.8 117.4 %reduce-scatter.5.cloned.1.call-start = ((), (), s32[]{:S(2)}) async-start(), calls=%async_computation.5 | async-start | bytes 1114112 | tf_op jit(solution)/shard_map/reduce_scatter | solution.py:175
Sparse Core Ops, SparseCore 0:
  10.2 40.6 all-gather.2
  53.0 36.8 all-gather.4
  113.9 56.3 reduce-scatter.2
  174.7 56.3 reduce-scatter.4

commit v2 on v1

--- a/solution.py
+++ b/solution.py
@@ -28,16 +28,14 @@
     meta_ref,
     q_ref,
     do_ref,
-    pk_ref,
-    pv_ref,
+    pkv_ref,
     ok_ref,
     ov_ref,
     out_ref,
     dq_ref,
     dok_ref,
     dov_ref,
-    dpk_ref,
-    dpv_ref,
+    dpkv_ref,
     k_all,
     v_all,
     bias,
@@ -65,8 +63,8 @@
 
     for i in range(entries):
         start = pl.multiple_of(slots_ref[i] * block_rows, block_rows)
-        k_all[i * block_rows : (i + 1) * block_rows, :] = pk_ref[pl.ds(start, block_rows), :]
-        v_all[i * block_rows : (i + 1) * block_rows, :] = pv_ref[pl.ds(start, block_rows), :]
+        k_all[i * block_rows : (i + 1) * block_rows, :] = pkv_ref[pl.ds(start, block_rows), :HD]
+        v_all[i * block_rows : (i + 1) * block_rows, :] = pkv_ref[pl.ds(start, block_rows), HD:]
     k_all[prefix:, :] = ok_ref[...]
     v_all[prefix:, :] = ov_ref[...]
     kk, vv = k_all[...], v_all[...]
@@ -99,29 +97,28 @@
     dv = dot(wl_all[...], do_all[...]).astype(jnp.bfloat16)
     dok_ref[...] = dk[prefix:, :]
     dov_ref[...] = dv[prefix:, :]
-    dpk_ref[...] = jnp.zeros_like(dpk_ref)
-    dpv_ref[...] = jnp.zeros_like(dpv_ref)
+    dpkv_ref[...] = jnp.zeros_like(dpkv_ref)
     for i in range(entries):
         start = pl.multiple_of(slots_ref[i] * block_rows, block_rows)
-        dpk_ref[pl.ds(start, block_rows), :] = dk[i * block_rows : (i + 1) * block_rows, :]
-        dpv_ref[pl.ds(start, block_rows), :] = dv[i * block_rows : (i + 1) * block_rows, :]
-
-
-def attention(slots, meta, queries, grads, keys, values, own_keys, own_values, block_rows):
+        dpkv_ref[pl.ds(start, block_rows), :HD] = dk[i * block_rows : (i + 1) * block_rows, :]
+        dpkv_ref[pl.ds(start, block_rows), HD:] = dv[i * block_rows : (i + 1) * block_rows, :]
+
+
+def attention(slots, meta, queries, grads, prompt, own_keys, own_values, block_rows):
     rows, width = queries.shape
-    slot_rows = keys.shape[0]
+    slot_rows = prompt.shape[0]
     total = slots.shape[0] * block_rows + rows
     wide = pl.BlockSpec((rows, GROUP * HD), lambda g, *_: (0, g))
     own = pl.BlockSpec((rows, HD), lambda g, *_: (0, g))
-    prompt = pl.BlockSpec((slot_rows, HD), lambda g, *_: (0, g))
+    shared = pl.BlockSpec((slot_rows, 2 * HD), lambda g, *_: (0, g))
     low = jnp.bfloat16
     return pl.pallas_call(
         functools.partial(attention_kernel, block_rows),
         grid_spec=pltpu.PrefetchScalarGridSpec(
             num_scalar_prefetch=2,
             grid=(KVH,),
-            in_specs=[wide, wide, prompt, prompt, own, own],
-            out_specs=[wide, wide, own, own, prompt, prompt],
+            in_specs=[wide, wide, shared, own, own],
+            out_specs=[wide, wide, own, own, shared],
             scratch_shapes=[
                 pltpu.VMEM((total, HD), low),
                 pltpu.VMEM((total, HD), low),
@@ -137,12 +134,191 @@
             jax.ShapeDtypeStruct((rows, width), low),
             jax.ShapeDtypeStruct((rows, KVH * HD), low),
             jax.ShapeDtypeStruct((rows, KVH * HD), low),
-            jax.ShapeDtypeStruct((slot_rows, KVH * HD), low),
-            jax.ShapeDtypeStruct((slot_rows, KVH * HD), low),
+            jax.ShapeDtypeStruct((slot_rows, 2 * KVH * HD), low),
         ],
-        compiler_params=pltpu.CompilerParams(vmem_limit_bytes=40 << 20),
+        compiler_params=pltpu.CompilerParams(vmem_limit_bytes=56 << 20),
         name="attention",
-    )(slots, meta, queries, grads, keys, values, own_keys, own_values)
+    )(slots, meta, queries, grads, prompt, own_keys, own_values)
+
+
+MESH = pl.DeviceIdType.MESH
+
+
+def plane(n):
+    me = lax.axis_index("seq")
+    z, y, c = me // 4, lax.rem(me // 2, 2), lax.rem(me, 2)
+
+    def index(dz, y, c):
+        return lax.rem(z + dz + n // 4, n // 4) * 4 + y * 2 + c
+
+    return me, y, c, index
+
+
+def greet(peers):
+    barrier = pltpu.get_barrier_semaphore()
+    for peer in peers:
+        pl.semaphore_signal(barrier, inc=1, device_id={"seq": peer}, device_id_type=MESH)
+    pl.semaphore_wait(barrier, len(peers))
+
+
+def gather_kernel(n, k_ref, v_ref, all_ref, zs, zr, ys, yr, cs, cr):
+    me, y, c, index = plane(n)
+    nz = n // 4
+    size = k_ref.shape[0]
+
+    def at(source):
+        return all_ref.at[pl.ds(pl.multiple_of(source * size, size), size), :]
+
+    for g in range(KVH):
+        all_ref[pl.ds(pl.multiple_of(me * size, size), size), 2 * g * HD : (2 * g + 1) * HD] = k_ref[
+            :, g * HD : (g + 1) * HD
+        ]
+        all_ref[pl.ds(pl.multiple_of(me * size, size), size), (2 * g + 1) * HD : (2 * g + 2) * HD] = v_ref[
+            :, g * HD : (g + 1) * HD
+        ]
+    across, partner = index(0, 1 - y, c), index(0, y, 1 - c)
+    greet([index(dz, y, c) for dz in range(1, nz)] + [across, partner])
+
+    def copy(source, send, recv, peer):
+        return pltpu.make_async_remote_copy(
+            src_ref=at(source),
+            dst_ref=at(source),
+            send_sem=send,
+            recv_sem=recv,
+            device_id={"seq": peer},
+            device_id_type=MESH,
+        )
+
+    started = []
+
+    def start(*args):
+        started.append(copy(*args))
+        started[-1].start()
+
+    for dz in range(1, nz):
+        start(me, zs.at[dz], zr.at[dz], index(dz, y, c))
+    for dz in range(nz):
+        source = index(-dz, y, c)
+        if dz:
+            copy(source, zs.at[dz], zr.at[dz], across).wait_recv()
+        start(source, ys.at[dz], yr.at[dz], across)
+        start(source, cs.at[dz], cr.at[dz], partner)
+    for dz in range(nz):
+        source = index(-dz, 1 - y, c)
+        copy(source, ys.at[dz], yr.at[dz], across).wait_recv()
+        start(source, cs.at[nz + dz], cr.at[nz + dz], partner)
+    for dz in range(nz):
+        copy(index(-dz, y, 1 - c), cs.at[dz], cr.at[dz], partner).wait_recv()
+        copy(index(-dz, 1 - y, 1 - c), cs.at[nz + dz], cr.at[nz + dz], partner).wait_recv()
+    for one in started:
+        one.wait_send()
+
+
+def gather(keys, values, n):
+    rows, width = keys.shape
+    nz = n // 4
+    vmem = pl.BlockSpec(memory_space=pltpu.VMEM)
+    dma = pltpu.SemaphoreType.DMA
+    return pl.pallas_call(
+        functools.partial(gather_kernel, n),
+        in_specs=[vmem, vmem],
+        out_specs=vmem,
+        out_shape=jax.ShapeDtypeStruct((n * rows, 2 * width), keys.dtype),
+        scratch_shapes=[dma((nz,)), dma((nz,)), dma((nz,)), dma((nz,)), dma((2 * nz,)), dma((2 * nz,))],
+        compiler_params=pltpu.CompilerParams(
+            collective_id=0, has_side_effects=True, vmem_limit_bytes=24 << 20
+        ),
+        name="gather",
+    )(keys, values)
+
+
+def scatter_kernel(n, t_ref, pk_ref, pv_ref, crecv, yrecv, zrecv, ysend, zsend, cs, cr, ys, yr, zs, zr):
+    me, y, c, index = plane(n)
+    nz = n // 4
+    size = pk_ref.shape[0]
+    across, partner = index(0, 1 - y, c), index(0, y, 1 - c)
+
+    def at(owner):
+        return t_ref.at[pl.ds(pl.multiple_of(owner * size, size), size), :]
+
+    def copy(source, target, send, recv, peer):
+        return pltpu.make_async_remote_copy(
+            src_ref=source,
+            dst_ref=target,
+            send_sem=send,
+            recv_sem=recv,
+            device_id={"seq": peer},
+            device_id_type=MESH,
+        )
+
+    greet([index(dz, y, c) for dz in range(1, nz)] + [across, partner])
+    order = list(range(1, nz)) + [0]
+    inside, over, along = {}, {}, {}
+    for dz in order:
+        for far in (1, 0):
+            slot = 2 * dz + far
+            owner = index(dz, 1 - y if far else y, 1 - c)
+            inside[slot] = copy(at(owner), crecv.at[slot], cs.at[slot], cr.at[slot], partner)
+            inside[slot].start()
+    for dz in order:
+        inside[2 * dz + 1].wait_recv()
+        mine = at(index(dz, 1 - y, c))[...].astype(jnp.float32)
+        ysend[dz] = (mine + crecv[2 * dz + 1].astype(jnp.float32)).astype(ysend.dtype)
+        over[dz] = copy(ysend.at[dz], yrecv.at[dz], ys.at[dz], yr.at[dz], across)
+        over[dz].start()
+    total = None
+    for dz in order:
+        inside[2 * dz].wait_recv()
+        mine = at(index(dz, y, c))[...].astype(jnp.float32) + crecv[2 * dz].astype(jnp.float32)
+        over[dz].wait_recv()
+        mine = mine + yrecv[dz].astype(jnp.float32)
+        if dz:
+            zsend[dz] = mine.astype(zsend.dtype)
+            along[dz] = copy(zsend.at[dz], zrecv.at[dz], zs.at[dz], zr.at[dz], index(dz, y, c))
+            along[dz].start()
+        else:
+            total = mine
+    for dz in range(1, nz):
+        along[dz].wait_recv()
+        total = total + zrecv[dz].astype(jnp.float32)
+    total = total.astype(pk_ref.dtype)
+    for g in range(KVH):
+        pk_ref[:, g * HD : (g + 1) * HD] = total[:, 2 * g * HD : (2 * g + 1) * HD]
+        pv_ref[:, g * HD : (g + 1) * HD] = total[:, (2 * g + 1) * HD : (2 * g + 2) * HD]
+    for one in [*inside.values(), *over.values(), *along.values()]:
+        one.wait_send()
+
+
+def scatter(terms, n):
+    rows, width = terms.shape[0] // n, terms.shape[1]
+    nz = n // 4
+    vmem = pl.BlockSpec(memory_space=pltpu.VMEM)
+    dma = pltpu.SemaphoreType.DMA
+    block = (nz, rows, width)
+    low = terms.dtype
+    return pl.pallas_call(
+        functools.partial(scatter_kernel, n),
+        in_specs=[vmem],
+        out_specs=[vmem, vmem],
+        out_shape=[jax.ShapeDtypeStruct((rows, width // 2), low)] * 2,
+        scratch_shapes=[
+            pltpu.VMEM((2 * nz, rows, width), low),
+            pltpu.VMEM(block, low),
+            pltpu.VMEM(block, low),
+            pltpu.VMEM(block, low),
+            pltpu.VMEM(block, low),
+            dma((2 * nz,)),
+            dma((2 * nz,)),
+            dma((nz,)),
+            dma((nz,)),
+            dma((nz,)),
+            dma((nz,)),
+        ],
+        compiler_params=pltpu.CompilerParams(
+            collective_id=1, has_side_effects=True, vmem_limit_bytes=40 << 20
+        ),
+        name="scatter",
+    )(terms)
 
 
 def per_device(
@@ -161,19 +337,13 @@
     count = lax.dynamic_index_in_dim(block_count, device_index, 0, keepdims=True)
     meta = jnp.concatenate([count, response_length])
     block_rows = prompt_keys.shape[0] // 2
-    all_keys = lax.all_gather(prompt_keys, "seq", axis=0, tiled=True)
-    all_values = lax.all_gather(prompt_values, "seq", axis=0, tiled=True)
-    out, dq, dok, dov, dpk, dpv = attention(
-        listed, meta, queries, output_grad, all_keys, all_values, response_keys, response_values, block_rows
+    n = lax.axis_size("seq")
+    prompt = gather(prompt_keys, prompt_values, n)
+    out, dq, dok, dov, terms = attention(
+        listed, meta, queries, output_grad, prompt, response_keys, response_values, block_rows
     )
-    return (
-        out,
-        dq,
-        dok,
-        dov,
-        lax.psum_scatter(dpk, "seq", scatter_dimension=0, tiled=True),
-        lax.psum_scatter(dpv, "seq", scatter_dimension=0, tiled=True),
-    )
+    dpk, dpv = scatter(terms, n)
+    return out, dq, dok, dov, dpk, dpv
 
 
 def solution(mesh):

time: 238 us -> 75.4 us (0.32)
  waiting for transfers between devices: 197 us -> 0 us
  Pallas kernels: 18 us -> 64.9 us
  between operations: 14.4 us -> 1.33 us
    reduce_scatter x2 -> x0, waiting for transfers between devices: 117 us -> none  [the longest x1 60.9 us: per_device(): lax.psum_scatter(dpv, 'seq', scatter_dimension=0, tiled=True)]
    all_gather x2 -> x0, waiting for transfers between devices: 78.6 us -> none  [the longest x1 39.5 us: per_device(): all_keys = lax.all_gather(prompt_keys, 'seq', axis=0, tiled=True)]
    pallas_call x0 -> x2, Pallas kernels: none -> 46.2 us  [the longest x1 23.4 us: gather(): pl.pallas_call(functools.partial(gather_kernel, n), in_specs=[vmem, vmem]...]
    unnamed x16 -> x12, local copies, waits for them, and re-layouts: 6.46 us -> 5.89 us
  transfers between devices with their start and end apart: 4 -> 0, of which waited for: 4 -> 0; matrix products, arithmetic and copies ran while one was open for 1% -> 0% of each run, Pallas kernels for 0% -> 0%
where the time goes in v2:
time: 75.4 us; the launch traced here: 75.1 us
  Pallas kernels  64.9 us (86%)
  local copies, waits for them, and re-layouts  7.64 us (10%)
  between operations  1.33 us (2%)
  other arithmetic  1.23 us (2%)
    pallas_call x1, Pallas kernels, gather(): pl.pallas_call(functools.partial(gather_kernel, n), in_specs=[vmem, vmem]...  23.4 us
    pallas_call x1, Pallas kernels, scatter(): pl.pallas_call(functools.partial(scatter_kernel, n), in_specs=[vmem], out...  22.8 us
    pallas_call x1, Pallas kernels, attention(): pl.pallas_call(functools.partial(attention_kernel, block_rows), grid_spec...  18.7 us
    unnamed x12, local copies, waits for them, and re-layouts  5.89 us

profile of v2, /device:TPU:0, one launch (start us, length us, event | category | flops | bytes accessed | tf_op | source)
XLA Modules:
  0.0 75.1 jit_solution(7849817440287522457)
XLA Ops:
  0.6 0.0 copy-start
  1.3 1.2 %dynamic_slice.9 = s32[1]{0:T(128)} dynamic-slice(s32[16]{0:T(128)} %param.16, s32[]{:T(128)S(6)} %select_n.6), dynamic_slice_sizes={1} | dynamic-slice | bytes 12 | tf_op jit(solution)/shard_map/jit(dynamic_index_in_dim)/dynamic_slice | solution.py:337
  2.5 1.2 %pad_add_fusion.meta_ref = s32[2]{0:T(128)} fusion(s32[1]{0:T(128)S(6)} %copy.17, s32[1]{0:T(128)} %dynamic_slice.9), kind=kLoop, calls=%fused_computation | loop fusion | flops 2 | bytes 16 | tf_op jit(solution)/shard_map/concatenate | solution.py:338
  3.8 0.0 copy-done
  3.8 0.5 dynamic-slice_bitcast_fusion.slots_ref
  4.3 0.0 copy-start.3
  4.3 0.8 %copy-done.3 = bf16[64,512]{1,0:T(8,128)(2,1)S(1)} copy-done((bf16[64,512]{1,0:T(8,128)(2,1)S(1)}, bf16[64,512]{1,0:T(8,128)(2,1)}, u32[]{:S(2)}) %copy-start.3) | copy-done | bytes 65560
  5.1 0.0 copy-start.4
  5.1 0.8 %copy-done.4 = bf16[64,512]{1,0:T(8,128)(2,1)S(1)} copy-done((bf16[64,512]{1,0:T(8,128)(2,1)S(1)}, bf16[64,512]{1,0:T(8,128)(2,1)}, u32[]{:S(2)}) %copy-start.4) | copy-done | bytes 65560
  6.0 23.4 %gather.1.pkv_ref = bf16[1024,1024]{1,0:T(8,128)(2,1)S(1)} custom-call(bf16[64,512]{1,0:T(8,128)(2,1)S(1)} %copy-done.3, bf16[64,512]{1,0:T(8,128)(2,1)S(1)} %copy-done.4), custom_call_target="tpu_custom_call" | custom-call | tf_op jit(solution)/shard_map/gather/pallas_call | solution.py:222
  29.4 0.0 copy-start.1
  29.4 1.3 %copy-done.1 = bf16[1024,1024]{1,0:T(8,128)(2,1)} copy-done((bf16[1024,1024]{1,0:T(8,128)(2,1)}, bf16[1024,1024]{1,0:T(8,128)(2,1)S(1)}, u32[]{:S(2)}) %copy-start.1) | copy-done | bytes 2097176
  30.7 18.7 %attention.1 = (bf16[128,4096]{1,0:T(8,128)(2,1)}, bf16[128,4096]{1,0:T(8,128)(2,1)}, bf16[128,512]{1,0:T(8,128)(2,1)}, bf16[128,512]{1,0:T(8,128)(2,1)}, bf16[1024,1024]{1,0:T(8,128)(2,1)}) custom-call(s32[12]{0:T(128)} %dynamic-slice_bitcast_fusion.slots_ref, s32[2]{0:T(128)} %pad_add_fusion.meta_ref, bf16[128,4096]{1,0:T(8,128)(2,1)} %q_ref.1, ...), custom_call_target="tpu_custom_call" | custom-call | tf_op jit(solution)/shard_map/attention/pallas_call | solution.py:115
  49.4 0.0 copy-start.2
  49.4 1.6 %copy-done.2 = bf16[1024,1024]{1,0:T(8,128)(2,1)S(1)} copy-done((bf16[1024,1024]{1,0:T(8,128)(2,1)S(1)}, bf16[1024,1024]{1,0:T(8,128)(2,1)}, u32[]{:S(2)}) %copy-start.2) | copy-done | bytes 2097176
  51.0 22.8 %scatter.1 = (bf16[64,512]{1,0:T(8,128)(2,1)S(1)}, bf16[64,512]{1,0:T(8,128)(2,1)S(1)}) custom-call(bf16[1024,1024]{1,0:T(8,128)(2,1)S(1)} %copy-done.2), custom_call_target="tpu_custom_call" | custom-call | tf_op jit(solution)/shard_map/scatter/pallas_call | solution.py:299
  73.8 0.6 copy.18
  74.4 0.6 copy.19
Async XLA Ops:
  0.6 3.1 %copy-start = (s32[16,12]{1,0:T(8,128)S(1)}, s32[16,12]{1,0:T(8,128)}, u32[]{:S(2)}) copy-start(s32[16,12]{1,0:T(8,128)} %param.15) | copy-start | bytes 2308
  4.3 0.8 %copy-start.3 = (bf16[64,512]{1,0:T(8,128)(2,1)S(1)}, bf16[64,512]{1,0:T(8,128)(2,1)}, u32[]{:S(2)}) copy-start(bf16[64,512]{1,0:T(8,128)(2,1)} %k_ref.1) | copy-start | bytes 196612
  5.1 0.8 %copy-start.4 = (bf16[64,512]{1,0:T(8,128)(2,1)S(1)}, bf16[64,512]{1,0:T(8,128)(2,1)}, u32[]{:S(2)}) copy-start(bf16[64,512]{1,0:T(8,128)(2,1)} %v_ref.1) | copy-start | bytes 196612
  29.4 1.4 %copy-start.1 = (bf16[1024,1024]{1,0:T(8,128)(2,1)}, bf16[1024,1024]{1,0:T(8,128)(2,1)S(1)}, u32[]{:S(2)}) copy-start(bf16[1024,1024]{1,0:T(8,128)(2,1)S(1)} %gather.1.pkv_ref) | copy-start | bytes 6291460
  49.4 1.6 %copy-start.2 = (bf16[1024,1024]{1,0:T(8,128)(2,1)S(1)}, bf16[1024,1024]{1,0:T(8,128)(2,1)}, u32[]{:S(2)}) copy-start(bf16[1024,1024]{1,0:T(8,128)(2,1)} %get-tuple-element.17.t_ref) | copy-start | bytes 6291460

commit v3 on v2

--- a/solution.py
+++ b/solution.py
@@ -13,6 +13,7 @@
 KVH = 4
 GROUP = QH // KVH
 
+PARTS = 2
 MASKED = -1e30
 
 
@@ -24,8 +25,9 @@
 
 def attention_kernel(
     block_rows,
-    slots_ref,
-    meta_ref,
+    list_ref,
+    count_ref,
+    length_ref,
     q_ref,
     do_ref,
     pkv_ref,
@@ -45,13 +47,17 @@
     do_all,
 ):
     rows = q_ref.shape[0]
-    entries = slots_ref.shape[0]
+    entries = list_ref.shape[1]
+    me = lax.axis_index("seq")
+    g = pl.program_id(0)
+    key_cols = pl.ds(pl.multiple_of(g * HD, HD), HD)
+    value_cols = pl.ds(pl.multiple_of((KVH + g) * HD, HD), HD)
     prefix = entries * block_rows
     keys = prefix + rows
     scaling = 1.0 / math.sqrt(HD)
-    count, length = meta_ref[0], meta_ref[1]
-
-    @pl.when(pl.program_id(0) == 0)
+    count, length = count_ref[me], length_ref[0]
+
+    @pl.when(g == 0)
     def _():
         key_row = lax.broadcasted_iota(jnp.int32, (prefix, 2 * rows), 0)
         bias[:prefix, :] = jnp.where(key_row < count * block_rows, 0.0, MASKED)
@@ -60,11 +66,12 @@
         own_bias = jnp.where((own <= tok) & (own < length), 0.0, MASKED)
         bias[prefix:, :rows] = own_bias
         bias[prefix:, rows:] = own_bias
+        dpkv_ref[...] = jnp.zeros_like(dpkv_ref)
 
     for i in range(entries):
-        start = pl.multiple_of(slots_ref[i] * block_rows, block_rows)
-        k_all[i * block_rows : (i + 1) * block_rows, :] = pkv_ref[pl.ds(start, block_rows), :HD]
-        v_all[i * block_rows : (i + 1) * block_rows, :] = pkv_ref[pl.ds(start, block_rows), HD:]
+        start = pl.multiple_of(list_ref[me, i] * block_rows, block_rows)
+        k_all[i * block_rows : (i + 1) * block_rows, :] = pkv_ref[pl.ds(start, block_rows), key_cols]
+        v_all[i * block_rows : (i + 1) * block_rows, :] = pkv_ref[pl.ds(start, block_rows), value_cols]
     k_all[prefix:, :] = ok_ref[...]
     v_all[prefix:, :] = ov_ref[...]
     kk, vv = k_all[...], v_all[...]
@@ -97,25 +104,24 @@
     dv = dot(wl_all[...], do_all[...]).astype(jnp.bfloat16)
     dok_ref[...] = dk[prefix:, :]
     dov_ref[...] = dv[prefix:, :]
-    dpkv_ref[...] = jnp.zeros_like(dpkv_ref)
     for i in range(entries):
-        start = pl.multiple_of(slots_ref[i] * block_rows, block_rows)
-        dpkv_ref[pl.ds(start, block_rows), :HD] = dk[i * block_rows : (i + 1) * block_rows, :]
-        dpkv_ref[pl.ds(start, block_rows), HD:] = dv[i * block_rows : (i + 1) * block_rows, :]
-
-
-def attention(slots, meta, queries, grads, prompt, own_keys, own_values, block_rows):
+        start = pl.multiple_of(list_ref[me, i] * block_rows, block_rows)
+        dpkv_ref[pl.ds(start, block_rows), key_cols] = dk[i * block_rows : (i + 1) * block_rows, :]
+        dpkv_ref[pl.ds(start, block_rows), value_cols] = dv[i * block_rows : (i + 1) * block_rows, :]
+
+
+def attention(block_list, block_count, length, queries, grads, prompt, own_keys, own_values, block_rows):
     rows, width = queries.shape
     slot_rows = prompt.shape[0]
-    total = slots.shape[0] * block_rows + rows
+    total = block_list.shape[1] * block_rows + rows
     wide = pl.BlockSpec((rows, GROUP * HD), lambda g, *_: (0, g))
     own = pl.BlockSpec((rows, HD), lambda g, *_: (0, g))
-    shared = pl.BlockSpec((slot_rows, 2 * HD), lambda g, *_: (0, g))
+    shared = pl.BlockSpec(memory_space=pltpu.VMEM)
     low = jnp.bfloat16
     return pl.pallas_call(
         functools.partial(attention_kernel, block_rows),
         grid_spec=pltpu.PrefetchScalarGridSpec(
-            num_scalar_prefetch=2,
+            num_scalar_prefetch=3,
             grid=(KVH,),
             in_specs=[wide, wide, shared, own, own],
             out_specs=[wide, wide, own, own, shared],
@@ -136,9 +142,9 @@
             jax.ShapeDtypeStruct((rows, KVH * HD), low),
             jax.ShapeDtypeStruct((slot_rows, 2 * KVH * HD), low),
         ],
-        compiler_params=pltpu.CompilerParams(vmem_limit_bytes=56 << 20),
+        compiler_params=pltpu.CompilerParams(vmem_limit_bytes=(40 << 20) - 4 * prompt.size),
         name="attention",
-    )(slots, meta, queries, grads, prompt, own_keys, own_values)
+    )(block_list, block_count, length, queries, grads, prompt, own_keys, own_values)
 
 
 MESH = pl.DeviceIdType.MESH
@@ -161,30 +167,33 @@
     pl.semaphore_wait(barrier, len(peers))
 
 
-def gather_kernel(n, k_ref, v_ref, all_ref, zs, zr, ys, yr, cs, cr):
+def gather_kernel(n, parts, k_ref, v_ref, all_ref, own_sem, zs, zr, ys, yr, cs, cr):
     me, y, c, index = plane(n)
     nz = n // 4
-    size = k_ref.shape[0]
-
-    def at(source):
-        return all_ref.at[pl.ds(pl.multiple_of(source * size, size), size), :]
-
-    for g in range(KVH):
-        all_ref[pl.ds(pl.multiple_of(me * size, size), size), 2 * g * HD : (2 * g + 1) * HD] = k_ref[
-            :, g * HD : (g + 1) * HD
-        ]
-        all_ref[pl.ds(pl.multiple_of(me * size, size), size), (2 * g + 1) * HD : (2 * g + 2) * HD] = v_ref[
-            :, g * HD : (g + 1) * HD
-        ]
+    size, width = k_ref.shape
+    step = size // parts
+
+    def at(source, part):
+        return all_ref.at[pl.ds(pl.multiple_of(source * size + part * step, step), step), :]
+
+    mine = pl.ds(pl.multiple_of(me * size, size), size)
+    loads = [
+        pltpu.make_async_copy(k_ref, all_ref.at[mine, :width], own_sem.at[0]),
+        pltpu.make_async_copy(v_ref, all_ref.at[mine, width:], own_sem.at[1]),
+    ]
+    for one in loads:
+        one.start()
     across, partner = index(0, 1 - y, c), index(0, y, 1 - c)
     greet([index(dz, y, c) for dz in range(1, nz)] + [across, partner])
-
-    def copy(source, send, recv, peer):
+    for one in loads:
+        one.wait()
+
+    def copy(source, part, send, recv, slot, peer):
         return pltpu.make_async_remote_copy(
-            src_ref=at(source),
-            dst_ref=at(source),
-            send_sem=send,
-            recv_sem=recv,
+            src_ref=at(source, part),
+            dst_ref=at(source, part),
+            send_sem=send.at[slot * parts + part],
+            recv_sem=recv.at[slot * parts + part],
             device_id={"seq": peer},
             device_id_type=MESH,
         )
@@ -195,21 +204,33 @@
         started.append(copy(*args))
         started[-1].start()
 
-    for dz in range(1, nz):
-        start(me, zs.at[dz], zr.at[dz], index(dz, y, c))
-    for dz in range(nz):
-        source = index(-dz, y, c)
-        if dz:
-            copy(source, zs.at[dz], zr.at[dz], across).wait_recv()
-        start(source, ys.at[dz], yr.at[dz], across)
-        start(source, cs.at[dz], cr.at[dz], partner)
-    for dz in range(nz):
+    for part in range(parts):
+        for dz in range(1, nz):
+            start(me, part, zs, zr, dz, index(dz, y, c))
+        start(me, part, ys, yr, 0, across)
+        start(me, part, cs, cr, 0, partner)
+
+    def over(dz, part):
         source = index(-dz, 1 - y, c)
-        copy(source, ys.at[dz], yr.at[dz], across).wait_recv()
-        start(source, cs.at[nz + dz], cr.at[nz + dz], partner)
-    for dz in range(nz):
-        copy(index(-dz, y, 1 - c), cs.at[dz], cr.at[dz], partner).wait_recv()
-        copy(index(-dz, 1 - y, 1 - c), cs.at[nz + dz], cr.at[nz + dz], partner).wait_recv()
+        copy(source, part, ys, yr, dz, across).wait_recv()
+        start(source, part, cs, cr, nz + dz, partner)
+
+    pending = []
+    for part in range(parts):
+        for dz in range(1, nz):
+            source = index(-dz, y, c)
+            copy(source, part, zs, zr, dz, across).wait_recv()
+            start(source, part, ys, yr, dz, across)
+            start(source, part, cs, cr, dz, partner)
+        for one in pending:
+            over(*one)
+        pending = [(dz, part) for dz in range(1, nz)] + [(0, part)]
+    for one in pending:
+        over(*one)
+    for part in range(parts):
+        for dz in range(nz):
+            copy(index(-dz, y, 1 - c), part, cs, cr, dz, partner).wait_recv()
+            copy(index(-dz, 1 - y, 1 - c), part, cs, cr, nz + dz, partner).wait_recv()
     for one in started:
         one.wait_send()
 
@@ -219,14 +240,16 @@
     nz = n // 4
     vmem = pl.BlockSpec(memory_space=pltpu.VMEM)
     dma = pltpu.SemaphoreType.DMA
+    parts = math.gcd(rows // 16, PARTS)
+    some, more = dma((parts * nz,)), dma((parts * 2 * nz,))
     return pl.pallas_call(
-        functools.partial(gather_kernel, n),
-        in_specs=[vmem, vmem],
+        functools.partial(gather_kernel, n, parts),
+        in_specs=[pl.BlockSpec(memory_space=pl.ANY)] * 2,
         out_specs=vmem,
         out_shape=jax.ShapeDtypeStruct((n * rows, 2 * width), keys.dtype),
-        scratch_shapes=[dma((nz,)), dma((nz,)), dma((nz,)), dma((nz,)), dma((2 * nz,)), dma((2 * nz,))],
+        scratch_shapes=[dma((2,)), some, some, some, some, more, more],
         compiler_params=pltpu.CompilerParams(
-            collective_id=0, has_side_effects=True, vmem_limit_bytes=24 << 20
+            collective_id=0, has_side_effects=True, vmem_limit_bytes=(50 << 20) - 4 * n * rows * width
         ),
         name="gather",
     )(keys, values)
@@ -282,9 +305,8 @@
         along[dz].wait_recv()
         total = total + zrecv[dz].astype(jnp.float32)
     total = total.astype(pk_ref.dtype)
-    for g in range(KVH):
-        pk_ref[:, g * HD : (g + 1) * HD] = total[:, 2 * g * HD : (2 * g + 1) * HD]
-        pv_ref[:, g * HD : (g + 1) * HD] = total[:, (2 * g + 1) * HD : (2 * g + 2) * HD]
+    pk_ref[...] = total[:, : pk_ref.shape[1]]
+    pv_ref[...] = total[:, pk_ref.shape[1] :]
     for one in [*inside.values(), *over.values(), *along.values()]:
         one.wait_send()
 
@@ -332,15 +354,19 @@
     block_count,
     response_length,
 ):
-    device_index = lax.axis_index("seq")
-    listed = lax.dynamic_index_in_dim(block_list, device_index, 0, keepdims=False)
-    count = lax.dynamic_index_in_dim(block_count, device_index, 0, keepdims=True)
-    meta = jnp.concatenate([count, response_length])
     block_rows = prompt_keys.shape[0] // 2
     n = lax.axis_size("seq")
     prompt = gather(prompt_keys, prompt_values, n)
     out, dq, dok, dov, terms = attention(
-        listed, meta, queries, output_grad, prompt, response_keys, response_values, block_rows
+        block_list,
+        block_count,
+        response_length,
+        queries,
+        output_grad,
+        prompt,
+        response_keys,
+        response_values,
+        block_rows,
     )
     dpk, dpv = scatter(terms, n)
     return out, dq, dok, dov, dpk, dpv

time: 75.4 us -> 69.3 us (0.919)
  local copies, waits for them, and re-layouts: 7.64 us -> 4.54 us
  Pallas kernels: 64.9 us -> 63 us
  other arithmetic: 1.23 us -> 0 us
    unnamed x12 -> x18, local copies, waits for them, and re-layouts: 5.89 us -> 4.54 us
    dynamic_slice x1 -> x0, local copies, waits for them, and re-layouts: 1.24 us -> none  [per_device(): lax.dynamic_index_in_dim(block_count, device_index, 0, keepdims=True)]
    concatenate x1 -> x0, other arithmetic: 1.23 us -> none  [per_device(): meta = jnp.concatenate([count, response_length])]
    pallas_call x1, Pallas kernels: 18.7 us -> 17.6 us  [attention(): pl.pallas_call(functools.partial(attention_kernel, block_rows), grid_spec...]
    pallas_call x1, Pallas kernels: 23.4 us -> 22.6 us  [gather(): pl.pallas_call(functools.partial(gather_kernel, n, parts), in_specs=[pl.B...]
where the time goes in v3:
time: 69.3 us; the launch traced here: 69.1 us
  Pallas kernels  63 us (91%)
  local copies, waits for them, and re-layouts  4.54 us (7%)
  between operations  1.52 us (2%)
    pallas_call x1, Pallas kernels, scatter(): pl.pallas_call(functools.partial(scatter_kernel, n), in_specs=[vmem], out...  22.8 us
    pallas_call x1, Pallas kernels, gather(): pl.pallas_call(functools.partial(gather_kernel, n, parts), in_specs=[pl.B...  22.6 us
    pallas_call x1, Pallas kernels, attention(): pl.pallas_call(functools.partial(attention_kernel, block_rows), grid_spec...  17.6 us
    unnamed x18, local copies, waits for them, and re-layouts  4.54 us

profile of v3, /device:TPU:0, one launch (start us, length us, event | category | flops | bytes accessed | tf_op | source)
XLA Modules:
  0.0 69.1 jit_solution(1521760569329489025)
XLA Ops:
  0.6 0.0 copy-start.1
  0.6 0.0 copy-start.2
  0.7 0.0 copy-start
  1.5 0.0 copy-start.4
  1.5 0.8 %copy-done.4 = bf16[64,512]{1,0:T(8,128)(2,1)S(1)} copy-done((bf16[64,512]{1,0:T(8,128)(2,1)S(1)}, bf16[64,512]{1,0:T(8,128)(2,1)}, u32[]{:S(2)}) %copy-start.4) | copy-done | bytes 65560
  2.3 0.0 copy-start.5
  2.3 0.8 %copy-done.5 = bf16[64,512]{1,0:T(8,128)(2,1)S(1)} copy-done((bf16[64,512]{1,0:T(8,128)(2,1)S(1)}, bf16[64,512]{1,0:T(8,128)(2,1)}, u32[]{:S(2)}) %copy-start.5) | copy-done | bytes 65560
  3.1 0.0 copy-start.7
  3.1 22.6 %gather.1.pkv_ref = bf16[1024,1024]{1,0:T(8,128)(2,1)S(1)} custom-call(bf16[64,512]{1,0:T(8,128)(2,1)S(1)} %copy-done.4, bf16[64,512]{1,0:T(8,128)(2,1)S(1)} %copy-done.5), custom_call_target="tpu_custom_call" | custom-call | tf_op jit(solution)/shard_map/gather/pallas_call | solution.py:245
  25.8 0.0 copy-done.1
  25.8 0.0 copy-done.2
  25.8 0.0 copy-done
  25.8 0.0 copy-done.7
  25.8 0.0 copy-start.3
  25.8 0.9 %copy-done.3 = bf16[128,512]{1,0:T(8,128)(2,1)S(1)} copy-done((bf16[128,512]{1,0:T(8,128)(2,1)S(1)}, bf16[128,512]{1,0:T(8,128)(2,1)}, u32[]{:S(2)}) %copy-start.3) | copy-done | bytes 131096
  26.7 0.0 copy-start.6
  26.7 0.7 %copy-done.6 = s32[16,12]{1,0:T(8,128)S(1)} copy-done((s32[16,12]{1,0:T(8,128)S(1)}, s32[16,12]{1,0:T(8,128)}, u32[]{:S(2)}) %copy-start.6) | copy-done | bytes 792
  27.4 17.6 %attention.1 = (bf16[128,4096]{1,0:T(8,128)(2,1)}, bf16[128,4096]{1,0:T(8,128)(2,1)}, bf16[128,512]{1,0:T(8,128)(2,1)}, bf16[128,512]{1,0:T(8,128)(2,1)}, bf16[1024,1024]{1,0:T(8,128)(2,1)S(1)}) custom-call(s32[16,12]{1,0:T(8,128)S(1)} %copy-done.6, s32[16]{0:T(128)S(1)} %copy-done.7, s32[1]{0:T(128)S(6)} %copy.17.length_ref, bf16[128,4096]{1,0:T(8,128)(2,1)S(1)} %copy-done, ...), custom_call_target="tpu_custom_call" | custom-call | tf_op jit(solution)/shard_map/attention/pallas_call | solution.py:121
  45.0 22.8 %scatter.1 = (bf16[64,512]{1,0:T(8,128)(2,1)S(1)}, bf16[64,512]{1,0:T(8,128)(2,1)S(1)}) custom-call(bf16[1024,1024]{1,0:T(8,128)(2,1)S(1)} %get-tuple-element.17.t_ref), custom_call_target="tpu_custom_call" | custom-call | tf_op jit(solution)/shard_map/scatter/pallas_call | solution.py:321
  67.8 0.6 copy.18
  68.5 0.6 copy.19
Async XLA Ops:
  0.6 25.2 %copy-start.1 = (bf16[128,4096]{1,0:T(8,128)(2,1)S(1)}, bf16[128,4096]{1,0:T(8,128)(2,1)}, u32[]{:S(2)}) copy-start(bf16[128,4096]{1,0:T(8,128)(2,1)} %do_ref.1) | copy-start | bytes 3145732
  0.6 25.2 %copy-start.2 = (bf16[128,512]{1,0:T(8,128)(2,1)S(1)}, bf16[128,512]{1,0:T(8,128)(2,1)}, u32[]{:S(2)}) copy-start(bf16[128,512]{1,0:T(8,128)(2,1)} %ok_ref.1) | copy-start | bytes 393220
  0.7 25.2 %copy-start = (bf16[128,4096]{1,0:T(8,128)(2,1)S(1)}, bf16[128,4096]{1,0:T(8,128)(2,1)}, u32[]{:S(2)}) copy-start(bf16[128,4096]{1,0:T(8,128)(2,1)} %q_ref.1) | copy-start | bytes 3145732
  1.5 0.8 %copy-start.4 = (bf16[64,512]{1,0:T(8,128)(2,1)S(1)}, bf16[64,512]{1,0:T(8,128)(2,1)}, u32[]{:S(2)}) copy-start(bf16[64,512]{1,0:T(8,128)(2,1)} %k_ref.1) | copy-start | bytes 196612
  2.3 0.8 %copy-start.5 = (bf16[64,512]{1,0:T(8,128)(2,1)S(1)}, bf16[64,512]{1,0:T(8,128)(2,1)}, u32[]{:S(2)}) copy-start(bf16[64,512]{1,0:T(8,128)(2,1)} %v_ref.1) | copy-start | bytes 196612
  3.1 22.7 %copy-start.7 = (s32[16]{0:T(128)S(1)}, s32[16]{0:T(128)}, u32[]{:S(2)}) copy-start(s32[16]{0:T(128)} %count_ref.1) | copy-start | bytes 196
  25.8 0.9 %copy-start.3 = (bf16[128,512]{1,0:T(8,128)(2,1)S(1)}, bf16[128,512]{1,0:T(8,128)(2,1)}, u32[]{:S(2)}) copy-start(bf16[128,512]{1,0:T(8,128)(2,1)} %ov_ref.1) | copy-start | bytes 393220
  26.7 0.7 %copy-start.6 = (s32[16,12]{1,0:T(8,128)S(1)}, s32[16,12]{1,0:T(8,128)}, u32[]{:S(2)}) copy-start(s32[16,12]{1,0:T(8,128)} %list_ref.1) | copy-start | bytes 2308

commit v4 on v3

--- a/solution.py
+++ b/solution.py
@@ -13,7 +13,7 @@
 KVH = 4
 GROUP = QH // KVH
 
-PARTS = 2
+PARTS = 4
 MASKED = -1e30
 
 
@@ -255,58 +255,64 @@
     )(keys, values)
 
 
-def scatter_kernel(n, t_ref, pk_ref, pv_ref, crecv, yrecv, zrecv, ysend, zsend, cs, cr, ys, yr, zs, zr):
+def scatter_kernel(n, parts, t_ref, pk_ref, pv_ref, crecv, yrecv, zrecv, ysend, zsend, cs, cr, ys, yr, zs, zr):
     me, y, c, index = plane(n)
     nz = n // 4
-    size = pk_ref.shape[0]
+    size, width = pk_ref.shape
+    step = size // parts
     across, partner = index(0, 1 - y, c), index(0, y, 1 - c)
 
-    def at(owner):
-        return t_ref.at[pl.ds(pl.multiple_of(owner * size, size), size), :]
-
-    def copy(source, target, send, recv, peer):
+    def at(owner, part):
+        return t_ref.at[pl.ds(pl.multiple_of(owner * size + part * step, step), step), :]
+
+    def copy(source, target, send, recv, slot, peer):
         return pltpu.make_async_remote_copy(
             src_ref=source,
-            dst_ref=target,
-            send_sem=send,
-            recv_sem=recv,
+            dst_ref=target.at[slot],
+            send_sem=send.at[slot],
+            recv_sem=recv.at[slot],
             device_id={"seq": peer},
             device_id_type=MESH,
         )
 
     greet([index(dz, y, c) for dz in range(1, nz)] + [across, partner])
-    order = list(range(1, nz)) + [0]
+    distances = sorted(range(1, nz), key=lambda dz: abs(2 * dz - nz)) + [0]
+    order = [(dz, part) for dz in distances for part in range(parts)]
     inside, over, along = {}, {}, {}
-    for dz in order:
-        for far in (1, 0):
-            slot = 2 * dz + far
+    for far in (1, 0):
+        for dz, part in order:
+            slot = (2 * dz + far) * parts + part
             owner = index(dz, 1 - y if far else y, 1 - c)
-            inside[slot] = copy(at(owner), crecv.at[slot], cs.at[slot], cr.at[slot], partner)
+            inside[slot] = copy(at(owner, part), crecv, cs, cr, slot, partner)
             inside[slot].start()
-    for dz in order:
-        inside[2 * dz + 1].wait_recv()
-        mine = at(index(dz, 1 - y, c))[...].astype(jnp.float32)
-        ysend[dz] = (mine + crecv[2 * dz + 1].astype(jnp.float32)).astype(ysend.dtype)
-        over[dz] = copy(ysend.at[dz], yrecv.at[dz], ys.at[dz], yr.at[dz], across)
-        over[dz].start()
-    total = None
-    for dz in order:
-        inside[2 * dz].wait_recv()
-        mine = at(index(dz, y, c))[...].astype(jnp.float32) + crecv[2 * dz].astype(jnp.float32)
-        over[dz].wait_recv()
-        mine = mine + yrecv[dz].astype(jnp.float32)
+    for dz, part in order:
+        slot, out = (2 * dz + 1) * parts + part, dz * parts + part
+        inside[slot].wait_recv()
+        mine = at(index(dz, 1 - y, c), part)[...].astype(jnp.float32)
+        ysend[out] = (mine + crecv[slot].astype(jnp.float32)).astype(ysend.dtype)
+        over[out] = copy(ysend.at[out], yrecv, ys, yr, out, across)
+        over[out].start()
+    totals = {}
+    for dz, part in order:
+        slot, out = 2 * dz * parts + part, dz * parts + part
+        inside[slot].wait_recv()
+        mine = at(index(dz, y, c), part)[...].astype(jnp.float32) + crecv[slot].astype(jnp.float32)
+        over[out].wait_recv()
+        mine = mine + yrecv[out].astype(jnp.float32)
         if dz:
-            zsend[dz] = mine.astype(zsend.dtype)
-            along[dz] = copy(zsend.at[dz], zrecv.at[dz], zs.at[dz], zr.at[dz], index(dz, y, c))
-            along[dz].start()
+            zsend[out] = mine.astype(zsend.dtype)
+            along[out] = copy(zsend.at[out], zrecv, zs, zr, out, index(dz, y, c))
+            along[out].start()
         else:
-            total = mine
-    for dz in range(1, nz):
-        along[dz].wait_recv()
-        total = total + zrecv[dz].astype(jnp.float32)
-    total = total.astype(pk_ref.dtype)
-    pk_ref[...] = total[:, : pk_ref.shape[1]]
-    pv_ref[...] = total[:, pk_ref.shape[1] :]
+            totals[part] = mine
+    for part in range(parts):
+        total = totals[part]
+        for dz in distances[:-1]:
+            along[dz * parts + part].wait_recv()
+            total = total + zrecv[dz * parts + part].astype(jnp.float32)
+        total = total.astype(pk_ref.dtype)
+        pk_ref[part * step : (part + 1) * step, :] = total[:, :width]
+        pv_ref[part * step : (part + 1) * step, :] = total[:, width:]
     for one in [*inside.values(), *over.values(), *along.values()]:
         one.wait_send()
 
@@ -316,25 +322,26 @@
     nz = n // 4
     vmem = pl.BlockSpec(memory_space=pltpu.VMEM)
     dma = pltpu.SemaphoreType.DMA
-    block = (nz, rows, width)
+    parts = math.gcd(rows // 16, 2)
+    block = (nz * parts, rows // parts, width)
     low = terms.dtype
     return pl.pallas_call(
-        functools.partial(scatter_kernel, n),
+        functools.partial(scatter_kernel, n, parts),
         in_specs=[vmem],
         out_specs=[vmem, vmem],
         out_shape=[jax.ShapeDtypeStruct((rows, width // 2), low)] * 2,
         scratch_shapes=[
-            pltpu.VMEM((2 * nz, rows, width), low),
+            pltpu.VMEM((2 * nz * parts, rows // parts, width), low),
             pltpu.VMEM(block, low),
             pltpu.VMEM(block, low),
             pltpu.VMEM(block, low),
             pltpu.VMEM(block, low),
-            dma((2 * nz,)),
-            dma((2 * nz,)),
-            dma((nz,)),
-            dma((nz,)),
-            dma((nz,)),
-            dma((nz,)),
+            dma((2 * nz * parts,)),
+            dma((2 * nz * parts,)),
+            dma((nz * parts,)),
+            dma((nz * parts,)),
+            dma((nz * parts,)),
+            dma((nz * parts,)),
         ],
         compiler_params=pltpu.CompilerParams(
             collective_id=1, has_side_effects=True, vmem_limit_bytes=40 << 20

time: 69.3 us -> 69.3 us (level)
    pallas_call x1, Pallas kernels: 22.8 us -> 21.9 us  [scatter(): pl.pallas_call(functools.partial(scatter_kernel, n, parts), in_specs=[vme...]
    pallas_call x1, Pallas kernels: 22.6 us -> 23.5 us  [gather(): pl.pallas_call(functools.partial(gather_kernel, n, parts), in_specs=[pl.B...]
where the time goes in v4:
time: 69.3 us; the launch traced here: 69.1 us
  Pallas kernels  63 us (91%)
  local copies, waits for them, and re-layouts  4.54 us (7%)
  between operations  1.52 us (2%)
    pallas_call x1, Pallas kernels, gather(): pl.pallas_call(functools.partial(gather_kernel, n, parts), in_specs=[pl.B...  23.5 us
    pallas_call x1, Pallas kernels, scatter(): pl.pallas_call(functools.partial(scatter_kernel, n, parts), in_specs=[vme...  21.9 us
    pallas_call x1, Pallas kernels, attention(): pl.pallas_call(functools.partial(attention_kernel, block_rows), grid_spec...  17.6 us
    unnamed x18, local copies, waits for them, and re-layouts  4.54 us

profile of v4, /device:TPU:0, one launch (start us, length us, event | category | flops | bytes accessed | tf_op | source)
XLA Modules:
  0.0 69.1 jit_solution(14274574050838562248)
XLA Ops:
  0.6 0.0 copy-start.1
  0.6 0.0 copy-start.2
  0.7 0.0 copy-start
  1.5 0.0 copy-start.4
  1.5 0.8 %copy-done.4 = bf16[64,512]{1,0:T(8,128)(2,1)S(1)} copy-done((bf16[64,512]{1,0:T(8,128)(2,1)S(1)}, bf16[64,512]{1,0:T(8,128)(2,1)}, u32[]{:S(2)}) %copy-start.4) | copy-done | bytes 65560
  2.3 0.0 copy-start.5
  2.3 0.8 %copy-done.5 = bf16[64,512]{1,0:T(8,128)(2,1)S(1)} copy-done((bf16[64,512]{1,0:T(8,128)(2,1)S(1)}, bf16[64,512]{1,0:T(8,128)(2,1)}, u32[]{:S(2)}) %copy-start.5) | copy-done | bytes 65560
  3.1 0.0 copy-start.7
  3.1 23.5 %gather.1.pkv_ref = bf16[1024,1024]{1,0:T(8,128)(2,1)S(1)} custom-call(bf16[64,512]{1,0:T(8,128)(2,1)S(1)} %copy-done.4, bf16[64,512]{1,0:T(8,128)(2,1)S(1)} %copy-done.5), custom_call_target="tpu_custom_call" | custom-call | tf_op jit(solution)/shard_map/gather/pallas_call | solution.py:245
  26.6 0.0 copy-done.1
  26.6 0.0 copy-done.2
  26.6 0.0 copy-done
  26.7 0.0 copy-done.7
  26.7 0.0 copy-start.3
  26.7 0.9 %copy-done.3 = bf16[128,512]{1,0:T(8,128)(2,1)S(1)} copy-done((bf16[128,512]{1,0:T(8,128)(2,1)S(1)}, bf16[128,512]{1,0:T(8,128)(2,1)}, u32[]{:S(2)}) %copy-start.3) | copy-done | bytes 131096
  27.6 0.0 copy-start.6
  27.6 0.7 %copy-done.6 = s32[16,12]{1,0:T(8,128)S(1)} copy-done((s32[16,12]{1,0:T(8,128)S(1)}, s32[16,12]{1,0:T(8,128)}, u32[]{:S(2)}) %copy-start.6) | copy-done | bytes 792
  28.3 17.6 %attention.1 = (bf16[128,4096]{1,0:T(8,128)(2,1)}, bf16[128,4096]{1,0:T(8,128)(2,1)}, bf16[128,512]{1,0:T(8,128)(2,1)}, bf16[128,512]{1,0:T(8,128)(2,1)}, bf16[1024,1024]{1,0:T(8,128)(2,1)S(1)}) custom-call(s32[16,12]{1,0:T(8,128)S(1)} %copy-done.6, s32[16]{0:T(128)S(1)} %copy-done.7, s32[1]{0:T(128)S(6)} %copy.17.length_ref, bf16[128,4096]{1,0:T(8,128)(2,1)S(1)} %copy-done, ...), custom_call_target="tpu_custom_call" | custom-call | tf_op jit(solution)/shard_map/attention/pallas_call | solution.py:121
  45.9 21.9 %scatter.1 = (bf16[64,512]{1,0:T(8,128)(2,1)S(1)}, bf16[64,512]{1,0:T(8,128)(2,1)S(1)}) custom-call(bf16[1024,1024]{1,0:T(8,128)(2,1)S(1)} %get-tuple-element.17.t_ref), custom_call_target="tpu_custom_call" | custom-call | tf_op jit(solution)/shard_map/scatter/pallas_call | solution.py:328
  67.8 0.6 copy.18
  68.4 0.6 copy.19
Async XLA Ops:
  0.6 26.0 %copy-start.1 = (bf16[128,4096]{1,0:T(8,128)(2,1)S(1)}, bf16[128,4096]{1,0:T(8,128)(2,1)}, u32[]{:S(2)}) copy-start(bf16[128,4096]{1,0:T(8,128)(2,1)} %do_ref.1) | copy-start | bytes 3145732
  0.6 26.0 %copy-start.2 = (bf16[128,512]{1,0:T(8,128)(2,1)S(1)}, bf16[128,512]{1,0:T(8,128)(2,1)}, u32[]{:S(2)}) copy-start(bf16[128,512]{1,0:T(8,128)(2,1)} %ok_ref.1) | copy-start | bytes 393220
  0.7 26.0 %copy-start = (bf16[128,4096]{1,0:T(8,128)(2,1)S(1)}, bf16[128,4096]{1,0:T(8,128)(2,1)}, u32[]{:S(2)}) copy-start(bf16[128,4096]{1,0:T(8,128)(2,1)} %q_ref.1) | copy-start | bytes 3145732
  1.5 0.8 %copy-start.4 = (bf16[64,512]{1,0:T(8,128)(2,1)S(1)}, bf16[64,512]{1,0:T(8,128)(2,1)}, u32[]{:S(2)}) copy-start(bf16[64,512]{1,0:T(8,128)(2,1)} %k_ref.1) | copy-start | bytes 196612
  2.3 0.8 %copy-start.5 = (bf16[64,512]{1,0:T(8,128)(2,1)S(1)}, bf16[64,512]{1,0:T(8,128)(2,1)}, u32[]{:S(2)}) copy-start(bf16[64,512]{1,0:T(8,128)(2,1)} %v_ref.1) | copy-start | bytes 196612
  3.1 23.5 %copy-start.7 = (s32[16]{0:T(128)S(1)}, s32[16]{0:T(128)}, u32[]{:S(2)}) copy-start(s32[16]{0:T(128)} %count_ref.1) | copy-start | bytes 196
  26.7 0.9 %copy-start.3 = (bf16[128,512]{1,0:T(8,128)(2,1)S(1)}, bf16[128,512]{1,0:T(8,128)(2,1)}, u32[]{:S(2)}) copy-start(bf16[128,512]{1,0:T(8,128)(2,1)} %ov_ref.1) | copy-start | bytes 393220
  27.6 0.7 %copy-start.6 = (s32[16,12]{1,0:T(8,128)S(1)}, s32[16,12]{1,0:T(8,128)}, u32[]{:S(2)}) copy-start(s32[16,12]{1,0:T(8,128)} %list_ref.1) | copy-start | bytes 2308

commit v5 on v4

--- a/solution.py
+++ b/solution.py
@@ -13,7 +13,7 @@
 KVH = 4
 GROUP = QH // KVH
 
-PARTS = 4
+PARTS = 2
 MASKED = -1e30
 
 
@@ -93,14 +93,14 @@
         ot = dot(vt, wl).astype(jnp.bfloat16)
         delta = (do2t.astype(jnp.float32) * ot.astype(jnp.float32)).sum(0, keepdims=True)
         dp = dot(vv, do2t)
-        ds = (w * (dp - delta) * scaling).astype(jnp.bfloat16)
+        ds = (w * (dp - delta)).astype(jnp.bfloat16)
         ds_all[:, span] = ds
-        dqt = dot(kt, ds).astype(jnp.bfloat16)
+        dqt = (dot(kt, ds) * scaling).astype(jnp.bfloat16)
         for j in range(2):
             h = 2 * pair + j
             out_ref[:, h * HD : (h + 1) * HD] = ot[:, j * rows : (j + 1) * rows].T
             dq_ref[:, h * HD : (h + 1) * HD] = dqt[:, j * rows : (j + 1) * rows].T
-    dk = dot(ds_all[...], q_all[...]).astype(jnp.bfloat16)
+    dk = (dot(ds_all[...], q_all[...]) * scaling).astype(jnp.bfloat16)
     dv = dot(wl_all[...], do_all[...]).astype(jnp.bfloat16)
     dok_ref[...] = dk[prefix:, :]
     dov_ref[...] = dv[prefix:, :]

time: 69.3 us -> 68.5 us (0.988)
  Pallas kernels: 63 us -> 62.2 us
    pallas_call x1, Pallas kernels: 23.5 us -> 22.6 us  [gather(): pl.pallas_call(functools.partial(gather_kernel, n, parts), in_specs=[pl.B...]
where the time goes in v5:
time: 68.5 us; the launch traced here: 68.2 us
  Pallas kernels  62.2 us (91%)
  local copies, waits for them, and re-layouts  4.54 us (7%)
  between operations  1.52 us (2%)
    pallas_call x1, Pallas kernels, gather(): pl.pallas_call(functools.partial(gather_kernel, n, parts), in_specs=[pl.B...  22.6 us
    pallas_call x1, Pallas kernels, scatter(): pl.pallas_call(functools.partial(scatter_kernel, n, parts), in_specs=[vme...  21.9 us
    pallas_call x1, Pallas kernels, attention(): pl.pallas_call(functools.partial(attention_kernel, block_rows), grid_spec...  17.6 us
    unnamed x18, local copies, waits for them, and re-layouts  4.54 us

profile of v5, /device:TPU:0, one launch (start us, length us, event | category | flops | bytes accessed | tf_op | source)
XLA Modules:
  0.0 68.2 jit_solution(7306520228316865465)
XLA Ops:
  0.6 0.0 copy-start.1
  0.6 0.0 copy-start.2
  0.7 0.0 copy-start
  1.5 0.0 copy-start.4
  1.5 0.8 %copy-done.4 = bf16[64,512]{1,0:T(8,128)(2,1)S(1)} copy-done((bf16[64,512]{1,0:T(8,128)(2,1)S(1)}, bf16[64,512]{1,0:T(8,128)(2,1)}, u32[]{:S(2)}) %copy-start.4) | copy-done | bytes 65560
  2.3 0.0 copy-start.5
  2.3 0.8 %copy-done.5 = bf16[64,512]{1,0:T(8,128)(2,1)S(1)} copy-done((bf16[64,512]{1,0:T(8,128)(2,1)S(1)}, bf16[64,512]{1,0:T(8,128)(2,1)}, u32[]{:S(2)}) %copy-start.5) | copy-done | bytes 65560
  3.1 0.0 copy-start.7
  3.1 22.6 %gather.1.pkv_ref = bf16[1024,1024]{1,0:T(8,128)(2,1)S(1)} custom-call(bf16[64,512]{1,0:T(8,128)(2,1)S(1)} %copy-done.4, bf16[64,512]{1,0:T(8,128)(2,1)S(1)} %copy-done.5), custom_call_target="tpu_custom_call" | custom-call | tf_op jit(solution)/shard_map/gather/pallas_call | solution.py:245
  25.8 0.0 copy-done.1
  25.8 0.0 copy-done.2
  25.8 0.0 copy-done
  25.8 0.0 copy-done.7
  25.8 0.0 copy-start.3
  25.8 0.9 %copy-done.3 = bf16[128,512]{1,0:T(8,128)(2,1)S(1)} copy-done((bf16[128,512]{1,0:T(8,128)(2,1)S(1)}, bf16[128,512]{1,0:T(8,128)(2,1)}, u32[]{:S(2)}) %copy-start.3) | copy-done | bytes 131096
  26.7 0.0 copy-start.6
  26.7 0.7 %copy-done.6 = s32[16,12]{1,0:T(8,128)S(1)} copy-done((s32[16,12]{1,0:T(8,128)S(1)}, s32[16,12]{1,0:T(8,128)}, u32[]{:S(2)}) %copy-start.6) | copy-done | bytes 792
  27.4 17.6 %attention.1 = (bf16[128,4096]{1,0:T(8,128)(2,1)}, bf16[128,4096]{1,0:T(8,128)(2,1)}, bf16[128,512]{1,0:T(8,128)(2,1)}, bf16[128,512]{1,0:T(8,128)(2,1)}, bf16[1024,1024]{1,0:T(8,128)(2,1)S(1)}) custom-call(s32[16,12]{1,0:T(8,128)S(1)} %copy-done.6, s32[16]{0:T(128)S(1)} %copy-done.7, s32[1]{0:T(128)S(6)} %copy.17.length_ref, bf16[128,4096]{1,0:T(8,128)(2,1)S(1)} %copy-done, ...), custom_call_target="tpu_custom_call" | custom-call | tf_op jit(solution)/shard_map/attention/pallas_call | solution.py:121
  45.0 21.9 %scatter.1 = (bf16[64,512]{1,0:T(8,128)(2,1)S(1)}, bf16[64,512]{1,0:T(8,128)(2,1)S(1)}) custom-call(bf16[1024,1024]{1,0:T(8,128)(2,1)S(1)} %get-tuple-element.17.t_ref), custom_call_target="tpu_custom_call" | custom-call | tf_op jit(solution)/shard_map/scatter/pallas_call | solution.py:328
  67.0 0.6 copy.18
  67.6 0.6 copy.19
Async XLA Ops:
  0.6 25.2 %copy-start.1 = (bf16[128,4096]{1,0:T(8,128)(2,1)S(1)}, bf16[128,4096]{1,0:T(8,128)(2,1)}, u32[]{:S(2)}) copy-start(bf16[128,4096]{1,0:T(8,128)(2,1)} %do_ref.1) | copy-start | bytes 3145732
  0.6 25.2 %copy-start.2 = (bf16[128,512]{1,0:T(8,128)(2,1)S(1)}, bf16[128,512]{1,0:T(8,128)(2,1)}, u32[]{:S(2)}) copy-start(bf16[128,512]{1,0:T(8,128)(2,1)} %ok_ref.1) | copy-start | bytes 393220
  0.7 25.2 %copy-start = (bf16[128,4096]{1,0:T(8,128)(2,1)S(1)}, bf16[128,4096]{1,0:T(8,128)(2,1)}, u32[]{:S(2)}) copy-start(bf16[128,4096]{1,0:T(8,128)(2,1)} %q_ref.1) | copy-start | bytes 3145732
  1.5 0.8 %copy-start.4 = (bf16[64,512]{1,0:T(8,128)(2,1)S(1)}, bf16[64,512]{1,0:T(8,128)(2,1)}, u32[]{:S(2)}) copy-start(bf16[64,512]{1,0:T(8,128)(2,1)} %k_ref.1) | copy-start | bytes 196612
  2.3 0.8 %copy-start.5 = (bf16[64,512]{1,0:T(8,128)(2,1)S(1)}, bf16[64,512]{1,0:T(8,128)(2,1)}, u32[]{:S(2)}) copy-start(bf16[64,512]{1,0:T(8,128)(2,1)} %v_ref.1) | copy-start | bytes 196612
  3.1 22.7 %copy-start.7 = (s32[16]{0:T(128)S(1)}, s32[16]{0:T(128)}, u32[]{:S(2)}) copy-start(s32[16]{0:T(128)} %count_ref.1) | copy-start | bytes 196
  25.8 0.9 %copy-start.3 = (bf16[128,512]{1,0:T(8,128)(2,1)S(1)}, bf16[128,512]{1,0:T(8,128)(2,1)}, u32[]{:S(2)}) copy-start(bf16[128,512]{1,0:T(8,128)(2,1)} %ov_ref.1) | copy-start | bytes 393220
  26.7 0.7 %copy-start.6 = (s32[16,12]{1,0:T(8,128)S(1)}, s32[16,12]{1,0:T(8,128)}, u32[]{:S(2)}) copy-start(s32[16,12]{1,0:T(8,128)} %list_ref.1) | copy-start | bytes 2308
